TPU v7x, 32 devices: a whole 2x2x4 slice. The times are simulated.
32 devices in a mesh: seq: 8 (over y, x, core), fsdp: 4 (over z).
Axes of the slice: x: 2, y: 2, z: 4, core: 2. Of those that a mesh axis runs over, the one named last changes fastest.
Arguments:
- latents: bfloat16 [8, 256, 3072], P('seq', None, 'fsdp'), may hold values from -6 to 6
- spatial_qkv: bfloat16 [3, 8, 256, 2048], P(None, 'seq', None, 'fsdp'), may hold values from -160 to 160
- spatial_out: bfloat16 [3072, 2048], P('seq', 'fsdp'), may hold values from -0.125 to 0.125
- temporal_qkv: bfloat16 [3072, 6144], P('seq', 'fsdp'), may hold values from -1.4072913 to 1.4072913
- temporal_out: bfloat16 [3072, 2048], P('seq', 'fsdp'), may hold values from -0.125 to 0.125
- mlp_in: bfloat16 [3072, 12288], P('seq', 'fsdp'), may hold values from -0.109375 to 0.109375
- mlp_out: bfloat16 [3072, 12288], P('seq', 'fsdp'), may hold values from -0.0546875 to 0.0546875
- upstream: bfloat16 [8, 256, 3072], P('seq'), may hold values from -6 to 6
Outputs:
- block_out: bfloat16 [8, 256, 3072], P('seq', None, 'fsdp')
- grad_latents: bfloat16 [8, 256, 3072], P('seq', None, 'fsdp')
- grad_spatial_qkv: bfloat16 [3, 8, 256, 2048], P(None, 'seq', None, 'fsdp')
- grad_spatial_out: float32 [3072, 2048], P('seq', 'fsdp')
- grad_temporal_qkv: float32 [3072, 6144], P('seq', 'fsdp')
- grad_temporal_out: float32 [3072, 2048], P('seq', 'fsdp')
- grad_mlp_in: float32 [3072, 12288], P('seq', 'fsdp')
- grad_mlp_out: float32 [3072, 12288], P('seq', 'fsdp')
All inputs are finite; a program needn't handle non-finite values.
Results may differ from a plain program's by a relative error of at most 0.03.
Values may be sent and summed in bfloat16 or wider, within the bound.
A program may use at most 192 MiB of HBM per device.

v0:
```python
import jax
import jax.numpy as jnp
from jax import lax
from jax.sharding import PartitionSpec as P

HD = 128


epsilon = 1e-06
grad_scale = 0.015625


def layer_norm(hidden):
    average = jnp.mean(hidden, axis=-1, keepdims=True)
    centred = hidden - average
    spread = jnp.mean(centred * centred, axis=-1, keepdims=True)
    return centred * lax.rsqrt(spread + epsilon)


def norm_back(hidden, incoming):
    average = jnp.mean(hidden, axis=-1, keepdims=True)
    centred = hidden - average
    spread = jnp.mean(centred * centred, axis=-1, keepdims=True)
    inverse = lax.rsqrt(spread + epsilon)
    normed = centred * inverse
    return inverse * (
        incoming
        - jnp.mean(incoming, axis=-1, keepdims=True)
        - normed * jnp.mean(incoming * normed, axis=-1, keepdims=True)
    )


def times_t(matrix, factor):
    return lax.dot_general(
        matrix, factor, (((1,), (1,)), ((), ())), preferred_element_type=jnp.float32
    )


def left_times(matrix, factor):
    return (
        lax.dot_general(
            matrix, factor, (((0,), (0,)), ((), ())), preferred_element_type=jnp.float32
        )
        * grad_scale
    )


def attend(query_rows, incoming_keys, value_rows):
    attention_logits = jnp.einsum(
        "otw,osw->ots", query_rows, incoming_keys, preferred_element_type=jnp.float32
    ) * query_rows.shape[-1] ** (-0.5)
    attention_probs = jax.nn.softmax(attention_logits, axis=-1).astype(jnp.bfloat16)
    return jnp.einsum(
        "hfj,hjt->hft", attention_probs, value_rows, preferred_element_type=jnp.float32
    ).astype(jnp.bfloat16)


def spatial(triple):
    frames = triple.shape[1]
    patches = triple.shape[2]
    columns = triple.shape[3]
    heads_here = columns // HD
    pieces = (
        triple.reshape(3, frames, patches, heads_here, HD)
        .transpose(0, 1, 3, 2, 4)
        .reshape(3, frames * heads_here, patches, HD)
    )
    result = attend(pieces[0], pieces[1], pieces[2])
    return (
        result.reshape(frames, heads_here, patches, HD)
        .transpose(0, 2, 1, 3)
        .reshape(frames * patches, columns)
    )


def temporal(triple_rows, frames, spot_count):
    heads_here = triple_rows.shape[1] // (3 * HD)
    pieces = (
        triple_rows.reshape(frames, spot_count, heads_here, 3, HD)
        .transpose(3, 1, 2, 0, 4)
        .reshape(3, spot_count * heads_here, frames, HD)
    )
    result = attend(pieces[0], pieces[1], pieces[2])
    return (
        result.reshape(spot_count, heads_here, frames, HD)
        .transpose(2, 0, 1, 3)
        .reshape(frames * spot_count, heads_here * HD)
    )


def smooth(pre_value):
    return jax.nn.gelu(pre_value, approximate=True)


def fetch_rows(weight):
    return lax.all_gather(weight, "seq", axis=0, tiled=True)


def widen(table):
    return lax.all_gather(table, "fsdp", axis=1, tiled=True)


def head_sum(terms):
    return lax.psum_scatter(
        terms.astype(jnp.bfloat16), "fsdp", scatter_dimension=1, tiled=True
    ).astype(jnp.float32)


def send_rows(grad_part):
    return lax.psum_scatter(
        grad_part.astype(jnp.bfloat16), "seq", scatter_dimension=0, tiled=True
    ).astype(jnp.float32)


def regroup(block):
    return lax.all_to_all(block, "seq", split_axis=0, concat_axis=1, tiled=True)


def to_positions(table, local_frames):
    devices = lax.axis_size("seq")
    row_count = table.shape[0]
    columns = table.shape[1]
    spot_count = row_count // (local_frames * devices)
    block = table.reshape(local_frames, devices, spot_count, columns).transpose(1, 0, 2, 3)
    return regroup(block).reshape(row_count, columns)


def to_frames(table, local_frames):
    devices = lax.axis_size("seq")
    row_count = table.shape[0]
    columns = table.shape[1]
    spot_count = row_count // (local_frames * devices)
    block = table.reshape(devices, local_frames, spot_count, columns)
    moved = regroup(block).reshape(devices, local_frames, spot_count, columns).transpose(1, 0, 2, 3)
    return moved.reshape(row_count, columns)


def body(latents, spatial_qkv, spatial_out, temporal_qkv, temporal_out, mlp_in, mlp_out, upstream):
    local_frames = latents.shape[0]
    patches = latents.shape[1]
    narrow = latents.shape[2]
    devices = lax.axis_size("seq")
    all_frames = local_frames * devices
    spot_count = patches // devices
    row_count = local_frames * patches
    spatial_output, spatial_back = jax.vjp(spatial, spatial_qkv)
    spatial_full = fetch_rows(spatial_out)
    first_mid = (
        latents.reshape(row_count, narrow).astype(jnp.float32)
        + head_sum(times_t(spatial_output, spatial_full))
    ).astype(jnp.bfloat16)
    first_wide = widen(to_positions(first_mid, local_frames)).astype(jnp.float32)
    first_norm = layer_norm(first_wide).astype(jnp.bfloat16)
    triple_full = fetch_rows(temporal_qkv)
    triple_rows = jnp.dot(first_norm, triple_full, preferred_element_type=jnp.float32).astype(
        jnp.bfloat16
    )
    temporal_result, temporal_back = jax.vjp(
        lambda triple: temporal(triple, all_frames, spot_count), triple_rows
    )
    frames_result = to_frames(temporal_result, local_frames)
    out_full = fetch_rows(temporal_out)
    second_mid = (
        first_mid.astype(jnp.float32) + head_sum(times_t(frames_result, out_full))
    ).astype(jnp.bfloat16)
    second_wide = widen(second_mid).astype(jnp.float32)
    second_norm = layer_norm(second_wide).astype(jnp.bfloat16)
    inner_full = fetch_rows(mlp_in)
    hidden_pre = jnp.dot(second_norm, inner_full, preferred_element_type=jnp.float32)
    hidden_act = smooth(hidden_pre).astype(jnp.bfloat16)
    outer_full = fetch_rows(mlp_out)
    block_out = (second_mid.astype(jnp.float32) + head_sum(times_t(hidden_act, outer_full))).astype(
        jnp.bfloat16
    )
    upstream_rows = upstream.reshape(row_count, upstream.shape[2])
    upstream_cols = lax.dynamic_slice_in_dim(
        upstream_rows, lax.axis_index("fsdp") * narrow, narrow, 1
    )
    act_grad = jnp.dot(upstream_rows, outer_full, preferred_element_type=jnp.float32)
    pre_grad = jax.vjp(smooth, hidden_pre)[1](act_grad)[0].astype(jnp.bfloat16)
    second_grad = (
        upstream_cols.astype(jnp.float32)
        + head_sum(norm_back(second_wide, times_t(pre_grad, inner_full)))
    ).astype(jnp.bfloat16)
    second_grad_wide = widen(second_grad)
    temporal_grad = to_positions(
        jnp.dot(second_grad_wide, out_full, preferred_element_type=jnp.float32).astype(
            jnp.bfloat16
        ),
        local_frames,
    )
    triple_grad = temporal_back(temporal_grad)[0]
    first_back = head_sum(norm_back(first_wide, times_t(triple_grad, triple_full))).astype(
        jnp.bfloat16
    )
    first_grad = (
        second_grad.astype(jnp.float32) + to_frames(first_back, local_frames).astype(jnp.float32)
    ).astype(jnp.bfloat16)
    first_grad_wide = widen(first_grad)
    spatial_grad = jnp.dot(
        first_grad_wide, spatial_full, preferred_element_type=jnp.float32
    ).astype(jnp.bfloat16)
    grad_spatial_qkv = spatial_back(spatial_grad)[0]
    grad_parts = (
        left_times(first_grad_wide, spatial_output),
        left_times(first_norm, triple_grad),
        left_times(second_grad_wide, frames_result),
        left_times(second_norm, pre_grad),
        left_times(upstream_rows, hidden_act),
    )
    grads = [send_rows(piece) for piece in grad_parts]
    return (
        block_out.reshape(local_frames, patches, narrow),
        first_grad.reshape(local_frames, patches, narrow),
        grad_spatial_qkv,
        grads[0],
        grads[1],
        grads[2],
        grads[3],
        grads[4],
    )


def solution(mesh):
    in_specs = (
        P("seq", None, "fsdp"),
        P(None, "seq", None, "fsdp"),
        P("seq", "fsdp"),
        P("seq", "fsdp"),
        P("seq", "fsdp"),
        P("seq", "fsdp"),
        P("seq", "fsdp"),
        P("seq", None, None),
    )
    out_specs = (
        P("seq", None, "fsdp"),
        P("seq", None, "fsdp"),
        P(None, "seq", None, "fsdp"),
        P("seq", "fsdp"),
        P("seq", "fsdp"),
        P("seq", "fsdp"),
        P("seq", "fsdp"),
        P("seq", "fsdp"),
    )
    return jax.shard_map(body, mesh=mesh, in_specs=in_specs, out_specs=out_specs, check_vma=False)
```

profile of v0, /device:TPU:0, one launch (start us, length us, event | category | flops | bytes accessed | tf_op | source)
XLA Modules:
  0.0 1202.0 jit_solution(3534248931221317268)
XLA Ops:
  7.9 1.3 fusion.74
  9.4 1.4 fusion.75
  11.6 33.3 %all-gather.10.cloned.1.call-done = bf16[3072,512]{1,0:T(8,128)(2,1)} async-done(((bf16[384,512]{1,0:T(8,128)(2,1)}), bf16[3072,512]{1,0:T(8,128)(2,1)}) %all-gather.10.cloned.1.call-update) | async-done | bytes 3145744 | tf_op jit(solution)/shard_map/all_gather | solution.py:96
  44.9 4.1 convolution_convert_fusion.2
  49.1 35.4 %reduce-scatter.13.cloned.1.call-done = bf16[256,768]{1,0:T(8,128)(2,1)} async-done(((bf16[256,3072]{1,0:T(8,128)(2,1)}), bf16[256,768]{1,0:T(8,128)(2,1)}) %reduce-scatter.13.cloned.1.call-update) | async-done | bytes 393232 | tf_op jit(solution)/shard_map/reduce_scatter | solution.py:104
  85.6 11.9 all_to_all.16
  98.7 33.2 %all-gather.12.cloned.1.call-done = bf16[256,3072]{1,0:T(8,128)(2,1)} async-done(((bf16[256,768]{1,0:T(8,128)(2,1)}), bf16[256,3072]{1,0:T(8,128)(2,1)}) %all-gather.12.cloned.1.call-update) | async-done | bytes 1572880 | tf_op jit(solution)/shard_map/all_gather | solution.py:100
  132.0 1.8 convert_reduce_fusion.1
  133.8 2.0 fusion.22
  135.8 55.7 %all-gather.14.cloned.1.call-done = bf16[3072,1536]{1,0:T(8,128)(2,1)} async-done(((bf16[384,1536]{1,0:T(8,128)(2,1)}), bf16[3072,1536]{1,0:T(8,128)(2,1)}) %all-gather.14.cloned.1.call-update) | async-done | bytes 9437200 | tf_op jit(solution)/shard_map/all_gather | solution.py:96
  191.4 7.2 convolution_convert_fusion.3
  198.6 2.8 reshape.173
  201.4 1.6 fusion.72
  206.2 3.4 all-to-all-start.1
  209.6 16.6 %all-gather.16.cloned.1.call-done = bf16[3072,512]{1,0:T(8,128)(2,1)} async-done(((bf16[384,512]{1,0:T(8,128)(2,1)}), bf16[3072,512]{1,0:T(8,128)(2,1)}) %all-gather.16.cloned.1.call-update) | async-done | bytes 3145744 | tf_op jit(solution)/shard_map/all_gather | solution.py:96
  226.2 4.1 convolution_convert_fusion.1
  230.4 34.8 %reduce-scatter.15.cloned.1.call-done = bf16[256,768]{1,0:T(8,128)(2,1)} async-done(((bf16[256,3072]{1,0:T(8,128)(2,1)}), bf16[256,768]{1,0:T(8,128)(2,1)}) %reduce-scatter.15.cloned.1.call-update) | async-done | bytes 393232 | tf_op jit(solution)/shard_map/reduce_scatter | solution.py:104
  265.2 1.8 add_convert_fusion.1
  268.8 34.7 %all-gather.18.cloned.1.call-done = bf16[256,3072]{1,0:T(8,128)(2,1)} async-done(((bf16[256,768]{1,0:T(8,128)(2,1)}), bf16[256,3072]{1,0:T(8,128)(2,1)}) %all-gather.18.cloned.1.call-update) | async-done | bytes 1572880 | tf_op jit(solution)/shard_map/all_gather | solution.py:100
  303.5 1.8 convert_reduce_fusion
  305.3 2.0 fusion.17
  307.3 95.7 %all-gather.20.cloned.1.call-done = bf16[3072,3072]{1,0:T(8,128)(2,1)} async-done(((bf16[384,3072]{1,0:T(8,128)(2,1)}), bf16[3072,3072]{1,0:T(8,128)(2,1)}) %all-gather.20.cloned.1.call-update) | async-done | bytes 18874384 | tf_op jit(solution)/shard_map/all_gather | solution.py:96
  403.0 10.9 fusion.66
  413.9 89.8 %all-gather.22.cloned.1.call-done = bf16[3072,3072]{1,0:T(8,128)(2,1)} async-done(((bf16[384,3072]{1,0:T(8,128)(2,1)}), bf16[3072,3072]{1,0:T(8,128)(2,1)}) %all-gather.22.cloned.1.call-update) | async-done | bytes 18874384 | tf_op jit(solution)/shard_map/all_gather | solution.py:96
  503.7 11.0 fusion.29
  514.7 10.3 fusion.71
  525.0 2.4 fusion.16
  527.5 35.4 %reduce-scatter.19.cloned.1.call-done = bf16[256,768]{1,0:T(8,128)(2,1)} async-done(((bf16[256,3072]{1,0:T(8,128)(2,1)}), bf16[256,768]{1,0:T(8,128)(2,1)}) %reduce-scatter.19.cloned.1.call-update) | async-done | bytes 393232 | tf_op jit(solution)/shard_map/reduce_scatter | solution.py:104
  562.8 2.0 fusion.52
  564.8 36.3 %all-gather.24.cloned.1.call-done = bf16[256,3072]{1,0:T(8,128)(2,1)} async-done(((bf16[256,768]{1,0:T(8,128)(2,1)}), bf16[256,3072]{1,0:T(8,128)(2,1)}) %all-gather.24.cloned.1.call-update) | async-done | bytes 1572880 | tf_op jit(solution)/shard_map/all_gather | solution.py:100
  601.1 4.0 convolution_convert_fusion.13
  605.2 4.0 all-to-all-start.2
  609.5 6.7 all-to-all-done.2
  616.1 1.7 reshape_reshape.3
  617.9 1.3 copy.62
  619.2 1.4 multiply_reduce_fusion
  620.6 1.5 fusion.42
  622.7 1.6 copy.101
  624.4 3.2 reshape.180
  627.6 5.7 fusion.70
  633.3 2.4 fusion.21
  635.8 32.5 %reduce-scatter.21.cloned.1.call-done = bf16[256,768]{1,0:T(8,128)(2,1)} async-done(((bf16[256,3072]{1,0:T(8,128)(2,1)}), bf16[256,768]{1,0:T(8,128)(2,1)}) %reduce-scatter.21.cloned.1.call-update) | async-done | bytes 393232 | tf_op jit(solution)/shard_map/reduce_scatter | solution.py:104
  668.2 12.0 all_to_all.17
  681.1 11.5 convolution_convert_fusion
  692.7 4.1 multiply_convert_fusion.3
  696.9 18.6 %all-gather.26.cloned.1.call-done = bf16[256,3072]{1,0:T(8,128)(2,1)} async-done(((bf16[256,768]{1,0:T(8,128)(2,1)}), bf16[256,3072]{1,0:T(8,128)(2,1)}) %all-gather.26.cloned.1.call-update) | async-done | bytes 1572880 | tf_op jit(solution)/shard_map/all_gather | solution.py:100
  715.5 4.1 multiply_convert_fusion.4
  719.7 6.5 multiply_convert_fusion.2
  727.6 12.7 %fusion.2 = bf16[3072,3072]{0,1:T(8,128)(2,1)} fusion(bf16[1,256,3072]{2,1,0:T(8,128)(2,1)S(1)} %copy-done.21, f32[256,3072]{1,0:T(8,128)} %fusion.66), kind=kOutput, calls=%fused_computation.5 | convolution fusion | flops 4857790464 | bytes 23592960 | tf_op jit(solution)/shard_map/dot_general | solution.py:41
  740.4 24.7 %copy.87 = bf16[3072,3072]{1,0:T(8,128)(2,1)} copy(bf16[3072,3072]{0,1:T(8,128)(2,1)} %fusion.2) | data formatting | bytes 37748736
  766.6 9.3 multiply_convert_fusion.1
  777.0 1.8 fusion.54
  778.8 22.0 %reduce-scatter.27.cloned.1.call-done = bf16[384,512]{1,0:T(8,128)(2,1)} async-done(((bf16[3072,512]{1,0:T(8,128)(2,1)}), bf16[384,512]{1,0:T(8,128)(2,1)}) %reduce-scatter.27.cloned.1.call-update) | async-done | bytes 393232 | tf_op jit(solution)/shard_map/reduce_scatter | solution.py:110
  800.9 2.0 convert_element_type.226
  802.9 3.5 convolution_convert_fusion.8
  810.5 40.9 %reduce-scatter.23.cloned.1.call-done = bf16[384,512]{1,0:T(8,128)(2,1)} async-done(((bf16[3072,512]{1,0:T(8,128)(2,1)}), bf16[384,512]{1,0:T(8,128)(2,1)}) %reduce-scatter.23.cloned.1.call-update) | async-done | bytes 393232 | tf_op jit(solution)/shard_map/reduce_scatter | solution.py:110
  851.3 2.0 convert_element_type.222
  853.3 77.9 %reduce-scatter.25.cloned.1.call-done = bf16[384,1536]{1,0:T(8,128)(2,1)} async-done(((bf16[3072,1536]{1,0:T(8,128)(2,1)}), bf16[384,1536]{1,0:T(8,128)(2,1)}) %reduce-scatter.25.cloned.1.call-update) | async-done | bytes 1179664 | tf_op jit(solution)/shard_map/reduce_scatter | solution.py:110
  931.2 3.0 convert_element_type.224
  934.2 126.7 %reduce-scatter.31.cloned.1.call-done = bf16[384,3072]{1,0:T(8,128)(2,1)} async-done(((bf16[3072,3072]{1,0:T(8,128)(2,1)}), bf16[384,3072]{1,0:T(8,128)(2,1)}) %reduce-scatter.31.cloned.1.call-update) | async-done | bytes 2359312
  1060.8 4.3 copy.88
  1065.1 4.5 copy.74
  1069.6 120.9 %reduce-scatter.29.cloned.1.call-done = bf16[384,3072]{1,0:T(8,128)(2,1)} async-done(((bf16[3072,3072]{1,0:T(8,128)(2,1)}), bf16[384,3072]{1,0:T(8,128)(2,1)}) %reduce-scatter.29.cloned.1.call-update) | async-done | bytes 2359312 | tf_op jit(solution)/shard_map/reduce_scatter | solution.py:110
  1190.6 4.4 convert_element_type.228
  (125 shorter events, 19.1 us)
Async XLA Ops:
  7.2 37.8 %all-gather.10.cloned.1.call-start = ((), (), s32[]{:S(2)}) async-start(), calls=%async_computation.14 | async-start | bytes 3538944 | tf_op jit(solution)/shard_map/all_gather | solution.py:96
  7.9 76.6 %reduce-scatter.13.cloned.1.call-start = ((), (), s32[]{:S(2)}) async-start(), calls=%async_computation.15 | async-start | bytes 1966080 | tf_op jit(solution)/shard_map/reduce_scatter | solution.py:104
  9.4 2.2 copy-start.7
  9.4 2.2 copy-start.17
  9.4 2.2 copy-start.19
  11.6 37.5 %copy-start.12 = (bf16[4,256,128]{1,2,0:T(8,128)(2,1)}, bf16[4,256,128]{1,2,0:T(8,128)(2,1)S(1)}, u32[]{:S(2)}) copy-start(bf16[4,256,128]{1,2,0:T(8,128)(2,1)S(1)} %convolution_convert_fusion.15) | copy-start | bytes 786436
  44.9 39.6 %copy-start.11 = (bf16[1,256,768]{2,1,0:T(8,128)(2,1)S(1)}, bf16[1,256,768]{2,1,0:T(8,128)(2,1)}, u32[]{:S(2)}) copy-start(bf16[1,256,768]{2,1,0:T(8,128)(2,1)} %param.8) | copy-start | bytes 1179652
  49.1 82.9 %all-gather.12.cloned.1.call-start = ((), (), s32[]{:S(2)}) async-start(), calls=%async_computation.16 | async-start | bytes 1966080 | tf_op jit(solution)/shard_map/all_gather | solution.py:100
  97.5 93.9 %all-gather.14.cloned.1.call-start = ((), (), s32[]{:S(2)}) async-start(), calls=%async_computation.17 | async-start | bytes 10616832 | tf_op jit(solution)/shard_map/all_gather | solution.py:96
  98.1 128.1 %all-gather.16.cloned.1.call-start = ((), (), s32[]{:S(2)}) async-start(), calls=%async_computation.18 | async-start | bytes 3538944 | tf_op jit(solution)/shard_map/all_gather | solution.py:96
  132.0 59.5 %copy-start = (bf16[256,3072]{1,0:T(8,128)(2,1)S(1)}, bf16[256,3072]{1,0:T(8,128)(2,1)}, u32[]{:S(2)}) copy-start(bf16[256,3072]{1,0:T(8,128)(2,1)} %all-gather.12.cloned.1.call-done) | copy-start | bytes 4718596
  203.6 26.7 %copy-start.14 = (bf16[1,32,4,8,128]{4,3,2,1,0:T(8,128)(2,1)}, bf16[1,32,4,8,128]{4,3,2,1,0:T(8,128)(2,1)S(1)}, u32[]{:S(2)}) copy-start(bf16[1,32,4,8,128]{4,3,2,1,0:T(8,128)(2,1)S(1)} %copy.55) | copy-start | bytes 786436
  204.0 26.4 %copy-start.16 = (bf16[1,32,4,8,128]{4,3,2,1,0:T(8,128)(2,1)}, bf16[1,32,4,8,128]{4,3,2,1,0:T(8,128)(2,1)S(1)}, u32[]{:S(2)}) copy-start(bf16[1,32,4,8,128]{4,3,2,1,0:T(8,128)(2,1)S(1)} %copy.56) | copy-start | bytes 786436
  204.5 0.8 copy-start.9
  206.2 20.0 %all-to-all-start.1 = ((bf16[8,1,32,512]{3,2,1,0:T(8,128)(2,1)}), bf16[8,1,32,512]{3,2,1,0:T(8,128)(2,1)S(1)}, u32[]{:S(2)}, u32[]{:S(2)}) async-start(bf16[8,1,32,512]{3,2,1,0:T(8,128)(2,1)} %bitcast.16), calls=%async_computation.2 | async-start | bytes 524288 | tf_op jit(solution)/shard_map/all_to_all | solution.py:116
  209.6 55.7 %reduce-scatter.15.cloned.1.call-start = ((), (), s32[]{:S(2)}) async-start(), calls=%async_computation.19 | async-start | bytes 1966080 | tf_op jit(solution)/shard_map/reduce_scatter | solution.py:104
  226.2 4.2 copy-start.4
  230.4 73.1 %all-gather.18.cloned.1.call-start = ((), (), s32[]{:S(2)}) async-start(), calls=%async_computation.20 | async-start | bytes 1966080 | tf_op jit(solution)/shard_map/all_gather | solution.py:100
  267.1 135.9 %all-gather.20.cloned.1.call-start = ((), (), s32[]{:S(2)}) async-start(), calls=%async_computation.21 | async-start | bytes 21233664 | tf_op jit(solution)/shard_map/all_gather | solution.py:96
  267.9 235.8 %all-gather.22.cloned.1.call-start = ((), (), s32[]{:S(2)}) async-start(), calls=%async_computation.22 | async-start | bytes 21233664 | tf_op jit(solution)/shard_map/all_gather | solution.py:96
  268.6 294.3 %reduce-scatter.19.cloned.1.call-start = ((), (), s32[]{:S(2)}) async-start(), calls=%async_computation.24 | async-start | bytes 1966080 | tf_op jit(solution)/shard_map/reduce_scatter | solution.py:104
  303.5 99.5 %copy-start.1 = (bf16[256,3072]{1,0:T(8,128)(2,1)S(1)}, bf16[256,3072]{1,0:T(8,128)(2,1)}, u32[]{:S(2)}) copy-start(bf16[256,3072]{1,0:T(8,128)(2,1)} %all-gather.18.cloned.1.call-done) | copy-start | bytes 4718596
  307.3 217.7 %copy-start.22 = (f32[256]{0:T(256)}, f32[256]{0:T(256)S(1)}, u32[]{:S(2)}) copy-start(f32[256]{0:T(256)S(1)} %add_rsqrt_fusion) | copy-start | bytes 3076
  514.7 10.3 copy-start.24
  527.4 73.7 %all-gather.24.cloned.1.call-start = ((), (), s32[]{:S(2)}) async-start(), calls=%async_computation.25 | async-start | bytes 1966080 | tf_op jit(solution)/shard_map/all_gather | solution.py:100
  605.2 11.0 all-to-all-start.2
  609.2 59.0 %reduce-scatter.21.cloned.1.call-start = ((), (), s32[]{:S(2)}) async-start(), calls=%async_computation.26 | async-start | bytes 1966080 | tf_op jit(solution)/shard_map/reduce_scatter | solution.py:104
  617.9 4.2 copy-start.10
  617.9 4.2 copy-start.15
  633.3 46.9 %copy-start.3 = (bf16[256,768]{1,0:T(8,128)(2,1)S(1)}, bf16[256,768]{1,0:T(8,128)(2,1)}, u32[]{:S(2)}) copy-start(bf16[256,768]{1,0:T(8,128)(2,1)} %fusion.52) | copy-start | bytes 1179652
  635.7 79.8 %all-gather.26.cloned.1.call-start = ((), (), s32[]{:S(2)}) async-start(), calls=%async_computation.27 | async-start | bytes 1966080 | tf_op jit(solution)/shard_map/all_gather | solution.py:100
  681.1 11.7 copy-start.5
  681.1 94.9 %reduce-scatter.17.cloned.1.call-start = ((), (), s32[]{:S(2)}) async-start(), calls=%async_computation.23 | async-start | bytes 1966080 | tf_op jit(solution)/shard_map/reduce_scatter | solution.py:104
  692.7 108.2 %reduce-scatter.27.cloned.1.call-start = ((), (), s32[]{:S(2)}) async-start(), calls=%async_computation.30 | async-start | bytes 3538944 | tf_op jit(solution)/shard_map/reduce_scatter | solution.py:110
  696.8 18.7 %copy-start.13 = (bf16[4,256,128]{1,2,0:T(8,128)(2,1)S(1)}, bf16[4,256,128]{1,2,0:T(8,128)(2,1)}, u32[]{:S(2)}) copy-start(bf16[4,256,128]{1,2,0:T(8,128)(2,1)} %copy-done.12) | copy-start | bytes 786436
  696.8 154.5 %reduce-scatter.23.cloned.1.call-start = ((), (), s32[]{:S(2)}) async-start(), calls=%async_computation.28 | async-start | bytes 3538944 | tf_op jit(solution)/shard_map/reduce_scatter | solution.py:110
  719.6 211.6 %reduce-scatter.25.cloned.1.call-start = ((), (), s32[]{:S(2)}) async-start(), calls=%async_computation.29 | async-start | bytes 10616832 | tf_op jit(solution)/shard_map/reduce_scatter | solution.py:110
  726.2 1.4 copy-start.21
  726.3 334.6 %reduce-scatter.31.cloned.1.call-start = ((), (), s32[]{:S(2)}) async-start(), calls=%async_computation.32 | async-start | bytes 21233664
  765.1 0.7 copy-start.23
  765.1 1.5 copy-start.25
  765.1 425.5 %reduce-scatter.29.cloned.1.call-start = ((), (), s32[]{:S(2)}) async-start(), calls=%async_computation.31 | async-start | bytes 21233664 | tf_op jit(solution)/shard_map/reduce_scatter | solution.py:110
  775.9 1.1 copy-start.2
  802.8 3.6 copy-start.6
  802.8 3.6 copy-start.8
  802.9 3.9 copy-start.18
  802.9 3.9 copy-start.20
Sparse Core Ops, SparseCore 0:
  9.9 35.0 all-gather.9
  49.2 35.2 reduce-scatter.12
  97.7 34.2 all-gather.11
  133.7 57.6 all-gather.13
  193.2 33.0 all-gather.15
  230.5 34.6 reduce-scatter.14
  267.4 36.0 all-gather.17
  305.4 97.5 all-gather.19
  404.9 98.7 all-gather.21
  527.5 35.2 reduce-scatter.18
  565.0 36.0 all-gather.23
  635.8 32.3 reduce-scatter.20
  681.2 34.2 all-gather.25
  718.2 34.1 reduce-scatter.16
  755.6 45.2 reduce-scatter.26
  805.1 46.2 reduce-scatter.22
  854.7 76.4 reduce-scatter.24
  934.7 126.1 reduce-scatter.30
  1064.5 126.0 reduce-scatter.28
where the time goes:
time: 1210 us; the launch traced here: 1200 us
  waiting for transfers between devices  950 us (79%)
  matrix products  118 us (10%)
  local copies, waits for them, and re-layouts  54.2 us (4%)
  other arithmetic  31.4 us (3%)
  blocking collectives  23.9 us (2%)
  between operations  15 us (1%)
    all_gather x5, waiting for transfers between devices, fetch_rows(): return lax.all_gather(weight, 'seq', axis=0, tiled=True)  291 us
    reduce_scatter x4, waiting for transfers between devices, send_rows(): lax.psum_scatter(grad_part.astype(jnp.bfloat16), 'seq', scatter_dimension...  262 us
    reduce_scatter x5, waiting for transfers between devices, head_sum(): lax.psum_scatter(terms.astype(jnp.bfloat16), 'fsdp', scatter_dimension=1,...  138 us
    unnamed x20, waiting for transfers between devices  130 us
    all_gather x4, waiting for transfers between devices, widen(): return lax.all_gather(table, 'fsdp', axis=1, tiled=True)  123 us
    unnamed x56, local copies, waits for them, and re-layouts  38.7 us
    dot_general x5, matrix products, left_times(): lax.dot_general(matrix, factor, (((0,), (0,)), ((), ())), preferred_eleme...  36.8 us
    dot_general x5, matrix products, times_t(): lax.dot_general(matrix, factor, (((1,), (1,)), ((), ())), preferred_eleme...  35.8 us
  transfers between devices with their start and end apart: 21, of which 19 were waited for; matrix products, arithmetic and copies ran while one was open for 11% of the time, Pallas kernels for 0%

commit v1 on v0

--- a/solution.py
+++ b/solution.py
@@ -97,13 +97,32 @@
 
 
 def widen(table):
-    return lax.all_gather(table, "fsdp", axis=1, tiled=True)
+    copies = jnp.broadcast_to(table[None], (lax.axis_size("fsdp"),) + table.shape)
+    return lax.all_to_all(copies, "fsdp", split_axis=0, concat_axis=2, tiled=True)[0]
 
 
 def head_sum(terms):
+    groups = lax.axis_size("fsdp")
+    moved = lax.all_to_all(
+        terms.astype(jnp.bfloat16), "fsdp", split_axis=1, concat_axis=0, tiled=True
+    )
+    return jnp.sum(
+        moved.reshape(groups, terms.shape[0], terms.shape[1] // groups).astype(jnp.float32), axis=0
+    )
+
+
+def late_sum(terms):
     return lax.psum_scatter(
         terms.astype(jnp.bfloat16), "fsdp", scatter_dimension=1, tiled=True
     ).astype(jnp.float32)
+
+
+def own_columns(table):
+    return lax.all_to_all(table, "seq", split_axis=1, concat_axis=0, tiled=True)
+
+
+def all_tokens(table):
+    return lax.all_gather(table, "seq", axis=0, tiled=True)
 
 
 def send_rows(grad_part):
@@ -169,7 +188,7 @@
     hidden_pre = jnp.dot(second_norm, inner_full, preferred_element_type=jnp.float32)
     hidden_act = smooth(hidden_pre).astype(jnp.bfloat16)
     outer_full = fetch_rows(mlp_out)
-    block_out = (second_mid.astype(jnp.float32) + head_sum(times_t(hidden_act, outer_full))).astype(
+    block_out = (second_mid.astype(jnp.float32) + late_sum(times_t(hidden_act, outer_full))).astype(
         jnp.bfloat16
     )
     upstream_rows = upstream.reshape(row_count, upstream.shape[2])
@@ -201,14 +220,13 @@
         first_grad_wide, spatial_full, preferred_element_type=jnp.float32
     ).astype(jnp.bfloat16)
     grad_spatial_qkv = spatial_back(spatial_grad)[0]
-    grad_parts = (
-        left_times(first_grad_wide, spatial_output),
-        left_times(first_norm, triple_grad),
-        left_times(second_grad_wide, frames_result),
-        left_times(second_norm, pre_grad),
-        left_times(upstream_rows, hidden_act),
-    )
-    grads = [send_rows(piece) for piece in grad_parts]
+    grads = (
+        send_rows(left_times(first_grad_wide, spatial_output)),
+        left_times(own_columns(first_norm), all_tokens(triple_grad)),
+        send_rows(left_times(second_grad_wide, frames_result)),
+        left_times(own_columns(second_norm), all_tokens(pre_grad)),
+        left_times(own_columns(upstream_rows), all_tokens(hidden_act)),
+    )
     return (
         block_out.reshape(local_frames, patches, narrow),
         first_grad.reshape(local_frames, patches, narrow),

time: 1210 us -> 905 us (0.75)
  waiting for transfers between devices: 950 us -> 395 us
  blocking collectives: 23.9 us -> 228 us
  starting transfers between devices: 8.87 us -> 35.4 us
  matrix products: 118 us -> 133 us
    reduce_scatter x4 -> x2, waiting for transfers between devices: 262 us -> 0.01 us  [send_rows(): lax.psum_scatter(grad_part.astype(jnp.bfloat16), 'seq', scatter_dimension...]
    all_gather x5, waiting for transfers between devices: 291 us -> 74.8 us  [fetch_rows(): return lax.all_gather(weight, 'seq', axis=0, tiled=True)]
    all_to_all x0 -> x5, blocking collectives: none -> 200 us  [the longest x3 118 us: widen(): lax.all_to_all(copies, 'fsdp', split_axis=0, concat_axis=2, tiled=True)[0]]
    all_to_all x0 -> x6, waiting for transfers between devices: none -> 180 us  [the longest x2 74.5 us: head_sum(): lax.all_to_all(terms.astype(jnp.bfloat16), 'fsdp', split_axis=1, concat_a...]
    reduce_scatter x5 -> x1, waiting for transfers between devices: 138 us -> 0.01 us  [late_sum(): lax.psum_scatter(terms.astype(jnp.bfloat16), 'fsdp', scatter_dimension=1,...]
    unnamed x20 -> x11, waiting for transfers between devices: 130 us -> 5.06 us
    all_to_all x0 -> x6, starting transfers between devices: none -> 26.7 us  [the longest x3 13 us: own_columns(): return lax.all_to_all(table, 'seq', split_axis=1, concat_axis=0, tiled=True)]
    unnamed x56 -> x65, local copies, waits for them, and re-layouts: 38.7 us -> 14.7 us
  transfers between devices with their start and end apart: 21 -> 19, of which waited for: 19 -> 12; matrix products, arithmetic and copies ran while one was open for 11% -> 19% of each run, Pallas kernels for 0% -> 0%
where the time goes in v1:
time: 905 us; the launch traced here: 895 us
  waiting for transfers between devices  395 us (44%)
  blocking collectives  228 us (25%)
  matrix products  133 us (15%)
  local copies, waits for them, and re-layouts  57.6 us (6%)
  starting transfers between devices  35.4 us (4%)
  other arithmetic  31.2 us (3%)
  between operations  14.8 us (2%)
    all_gather x3, waiting for transfers between devices, all_tokens(): return lax.all_gather(table, 'seq', axis=0, tiled=True)  128 us
    all_to_all x3, blocking collectives, widen(): lax.all_to_all(copies, 'fsdp', split_axis=0, concat_axis=2, tiled=True)[0]  118 us
    all_to_all x2, blocking collectives, head_sum(): lax.all_to_all(terms.astype(jnp.bfloat16), 'fsdp', split_axis=1, concat_a...  81.2 us
    all_gather x5, waiting for transfers between devices, fetch_rows(): return lax.all_gather(weight, 'seq', axis=0, tiled=True)  74.8 us
    all_to_all x2, waiting for transfers between devices, head_sum(): lax.all_to_all(terms.astype(jnp.bfloat16), 'fsdp', split_axis=1, concat_a...  74.5 us
    all_to_all x3, waiting for transfers between devices, own_columns(): return lax.all_to_all(table, 'seq', split_axis=1, concat_axis=0, tiled=True)  70.4 us
    dot_general x5, matrix products, left_times(): lax.dot_general(matrix, factor, (((0,), (0,)), ((), ())), preferred_eleme...  36.1 us
    dot_general x5, matrix products, times_t(): lax.dot_general(matrix, factor, (((1,), (1,)), ((), ())), preferred_eleme...  35.6 us
  transfers between devices with their start and end apart: 19, of which 12 were waited for; matrix products, arithmetic and copies ran while one was open for 19% of the time, Pallas kernels for 0%

profile of v1, /device:TPU:0, one launch (start us, length us, event | category | flops | bytes accessed | tf_op | source)
XLA Modules:
  0.0 894.9 jit_solution(18003266027734006618)
XLA Ops:
  13.1 31.8 %all-gather.9.cloned.1.call-done = bf16[3072,512]{1,0:T(8,128)(2,1)} async-done(((bf16[384,512]{1,0:T(8,128)(2,1)}), bf16[3072,512]{1,0:T(8,128)(2,1)}) %all-gather.9.cloned.1.call-update) | async-done | bytes 3145744 | tf_op jit(solution)/shard_map/all_gather | solution.py:96
  44.9 2.9 convolution_convert_fusion.2
  48.0 41.9 %all_to_all.187 = bf16[256,4,768]{2,0,1:T(8,128)(2,1)S(1)} all-to-all(bf16[256,4,768]{2,0,1:T(8,128)(2,1)S(1)} %bitcast.225), channel_id=1, replica_groups=mesh['seq'=8,'fsdp'=4] {'fsdp'}, dimensions={1} | all-to-all | bytes 3145728 | tf_op jit(solution)/shard_map/all_to_all | solution.py:106
  90.3 15.4 %all_to_all.188 = bf16[8,1,32,768]{3,2,1,0:T(8,128)(2,1)S(1)} all-to-all(bf16[8,1,32,768]{3,2,1,0:T(8,128)(2,1)S(1)} %add_convert_fusion.2), channel_id=1, replica_groups=mesh['seq'=8,'fsdp'=4] {'seq'}, dimensions={0} | all-to-all | bytes 786432 | tf_op jit(solution)/shard_map/all_to_all | solution.py:135
  106.0 38.5 %all_to_all.189 = bf16[4,256,768]{1,2,0:T(8,128)(2,1)S(1)} all-to-all(bf16[4,256,768]{1,2,0:T(8,128)(2,1)S(1)} %broadcast_in_dim.37), channel_id=1, replica_groups=mesh['seq'=8,'fsdp'=4] {'fsdp'}, dimensions={0} | all-to-all | bytes 3145728 | tf_op jit(solution)/shard_map/all_to_all | solution.py:101
  145.9 2.4 copy.130
  148.2 1.8 convert_reduce_fusion.4
  150.1 1.9 fusion.12
  152.0 10.2 %convolution_convert_fusion.3 = bf16[256,1536]{1,0:T(8,128)(2,1)} fusion(bf16[3072,1536]{1,0:T(8,128)(2,1)} %all-gather.11.cloned.1.call-done, f32[256,3072]{1,0:T(8,128)} %copy.130, f32[256]{0:T(256)S(1)} %add_rsqrt_fusion.1, f32[256]{0:T(256)S(1)} %broadcast_multiply_fusion.5), kind=kOutput, calls=%fused_computation.37 | convolution fusion | flops 2418671616 | bytes 13371392 | tf_op jit(solution)/shard_map/dot_general | solution.py:174
  162.2 3.6 reshape.293
  165.7 3.8 fusion.61
  172.6 2.9 fusion.65
  177.8 1.8 reshape.295
  179.6 4.2 all-to-all-start.3
  183.8 6.9 all-to-all-done.3
  190.8 3.8 convolution_convert_fusion.1
  194.7 39.3 %all_to_all.190 = bf16[256,4,768]{2,0,1:T(8,128)(2,1)S(1)} all-to-all(bf16[256,4,768]{2,0,1:T(8,128)(2,1)S(1)} %bitcast.226), channel_id=1, replica_groups=mesh['seq'=8,'fsdp'=4] {'fsdp'}, dimensions={1} | all-to-all | bytes 3145728 | tf_op jit(solution)/shard_map/all_to_all | solution.py:106
  237.3 39.0 %all_to_all.191 = bf16[4,256,768]{1,2,0:T(8,128)(2,1)S(1)} all-to-all(bf16[4,256,768]{1,2,0:T(8,128)(2,1)S(1)} %broadcast_in_dim.39), channel_id=1, replica_groups=mesh['seq'=8,'fsdp'=4] {'fsdp'}, dimensions={0} | all-to-all | bytes 3145728 | tf_op jit(solution)/shard_map/all_to_all | solution.py:101
  277.5 1.9 convert_element_type.340
  279.4 3.5 copy.131
  282.9 1.8 convert_reduce_fusion.3
  284.8 1.9 fusion.10
  286.7 15.5 %multiply_convert_fusion.6 = (bf16[256,3072]{1,0:T(8,128)(2,1)}, f32[256,3072]{1,0:T(8,128)}) fusion(bf16[3072,3072]{1,0:T(8,128)(2,1)} %all-gather.15.cloned.1.call-done, f32[256,3072]{1,0:T(8,128)} %copy.131, f32[256]{0:T(256)S(1)} %add_rsqrt_fusion, f32[256]{0:T(256)S(1)} %broadcast_multiply_fusion.4), kind=kOutput, calls=%fused_computation.31 | convolution fusion | flops 4841275392 | bytes 26740736 | tf_op jit(solution)/shard_map/dot_general | solution.py:188
  302.2 42.9 %all-gather.17.cloned.1.call-done = bf16[3072,3072]{1,0:T(8,128)(2,1)} async-done(((bf16[384,3072]{1,0:T(8,128)(2,1)}), bf16[3072,3072]{1,0:T(8,128)(2,1)}) %all-gather.17.cloned.1.call-update) | async-done | bytes 18874384 | tf_op jit(solution)/shard_map/all_gather | solution.py:96
  345.1 12.0 %fusion.8 = bf16[256,3072]{1,0:T(8,128)(2,1)} fusion(f32[256,3072]{1,0:T(8,128)} %get-tuple-element.59, bf16[3072,3072]{1,0:T(8,128)(2,1)} %all-gather.17.cloned.1.call-done, bf16[1,256,3072]{2,1,0:T(8,128)(2,1)} %param.15), kind=kOutput, calls=%fused_computation.17 | convolution fusion | flops 4847566848 | bytes 25165824 | tf_op jit(solution)/shard_map/dot_general | solution.py:198
  357.1 10.7 %fusion.60 = (f32[256]{0:T(256)S(1)}, f32[256]{0:T(256)S(1)}, f32[256,3072]{1,0:T(8,128)S(1)}) fusion(f32[256]{0:T(256)S(1)} %add_rsqrt_fusion, f32[256,3072]{1,0:T(8,128)} %copy.131, f32[256]{0:T(256)S(1)} %broadcast_multiply_fusion.4, bf16[256,3072]{1,0:T(8,128)(2,1)} %fusion.8, bf16[3072,3072]{1,0:T(8,128)(2,1)} %all-gather.15.cloned.1.call-done), kind=kOutput, calls=%fused_computation.128 | convolution fusion | flops 4835770368 | bytes 26742784 | tf_op jit(solution)/shard_map/dot_general | solution.py:34
  370.4 5.0 all-to-all-start.6
  375.4 37.5 %all-to-all-done.6 = bf16[256,4,768]{2,0,1:T(8,128)(2,1)} async-done(((bf16[256,4,768]{2,0,1:T(8,128)(2,1)}), bf16[256,4,768]{2,0,1:T(8,128)(2,1)}, u32[]{:S(2)}, u32[]{:S(2)}) %all-to-all-start.6) | async-done | bytes 1572896 | tf_op jit(solution)/shard_map/all_to_all | solution.py:106
  416.6 2.2 broadcast_in_dim.82
  418.8 4.4 all-to-all-start.7
  424.7 35.1 %all-to-all-done.7 = bf16[4,256,768]{1,2,0:T(8,128)(2,1)} async-done(((bf16[4,256,768]{1,2,0:T(8,128)(2,1)}), bf16[4,256,768]{1,2,0:T(8,128)(2,1)}, u32[]{:S(2)}, u32[]{:S(2)}) %all-to-all-start.7) | async-done | bytes 1572896 | tf_op jit(solution)/shard_map/all_to_all | solution.py:101
  459.8 4.1 convolution_convert_fusion.13
  463.9 4.1 all-to-all-start.8
  468.0 10.3 %convolution_convert_fusion = bf16[256,3072]{1,0:T(8,128)(2,1)} fusion(bf16[256,3072]{1,0:T(8,128)(2,1)} %get-tuple-element.58, bf16[3072,3072]{1,0:T(8,128)(2,1)} %all-gather.17.cloned.1.call-done), kind=kOutput, calls=%fused_computation.8 | convolution fusion | flops 4832624640 | bytes 22020096 | tf_op jit(solution)/shard_map/dot_general | solution.py:34
  486.8 3.2 reshape.300
  490.0 7.8 fusion.59
  500.4 4.3 all-to-all-start.9
  504.8 4.0 multiply_convert_fusion
  508.9 37.0 %all-to-all-done.9 = bf16[256,4,768]{2,0,1:T(8,128)(2,1)} async-done(((bf16[256,4,768]{2,0,1:T(8,128)(2,1)}), bf16[256,4,768]{2,0,1:T(8,128)(2,1)}, u32[]{:S(2)}, u32[]{:S(2)}) %all-to-all-start.9) | async-done | bytes 1572896 | tf_op jit(solution)/shard_map/all_to_all | solution.py:106
  545.9 2.5 reduce_sum.197
  548.5 13.2 %all_to_all.192 = bf16[8,1,32,768]{3,2,1,0:T(8,128)(2,1)S(1)} all-to-all(bf16[8,1,32,768]{3,2,1,0:T(8,128)(2,1)} %bitcast.239), channel_id=1, replica_groups=mesh['seq'=8,'fsdp'=4] {'seq'}, dimensions={0} | all-to-all | bytes 786432 | tf_op jit(solution)/shard_map/all_to_all | solution.py:135
  563.8 40.8 %all_to_all.193 = bf16[4,256,768]{1,2,0:T(8,128)(2,1)S(1)} all-to-all(bf16[4,256,768]{1,2,0:T(8,128)(2,1)S(1)} %broadcast_in_dim.89), channel_id=1, replica_groups=mesh['seq'=8,'fsdp'=4] {'fsdp'}, dimensions={0} | all-to-all | bytes 3145728 | tf_op jit(solution)/shard_map/all_to_all | solution.py:101
  605.8 2.7 multiply_convert_fusion.1
  610.5 2.7 copy.116
  613.3 4.3 all-to-all-start.14
  619.1 27.6 %all-to-all-done.14 = bf16[256,8,384]{0,2,1:T(8,128)(2,1)} async-done(((bf16[256,8,384]{0,2,1:T(8,128)(2,1)}), bf16[256,8,384]{0,2,1:T(8,128)(2,1)}, u32[]{:S(2)}, u32[]{:S(2)}) %all-to-all-start.14) | async-done | bytes 1572896 | tf_op jit(solution)/shard_map/all_to_all | solution.py:121
  646.7 4.3 all-to-all-start.12
  652.5 22.3 %all-to-all-done.12 = bf16[256,8,384]{0,2,1:T(8,128)(2,1)} async-done(((bf16[256,8,384]{0,2,1:T(8,128)(2,1)}), bf16[256,8,384]{0,2,1:T(8,128)(2,1)}, u32[]{:S(2)}, u32[]{:S(2)}) %all-to-all-start.12) | async-done | bytes 1572896 | tf_op jit(solution)/shard_map/all_to_all | solution.py:121
  674.8 4.3 all-to-all-start.13
  679.2 2.6 copy.117
  681.8 2.0 copy.114
  683.8 20.5 %all-to-all-done.13 = bf16[256,8,384]{0,2,1:T(8,128)(2,1)} async-done(((bf16[256,8,384]{0,2,1:T(8,128)(2,1)}), bf16[256,8,384]{0,2,1:T(8,128)(2,1)}, u32[]{:S(2)}, u32[]{:S(2)}) %all-to-all-start.13) | async-done | bytes 1572896 | tf_op jit(solution)/shard_map/all_to_all | solution.py:121
  704.2 2.6 copy.115
  706.8 1.9 fusion.47
  708.7 2.0 convert_element_type.324
  710.7 3.4 convolution_convert_fusion.8
  722.5 2.0 convert_element_type.319
  724.5 4.6 all-gather.19.cloned.1.call-done
  729.2 6.8 convolution_multiply_fusion.1
  736.0 67.1 %all-gather.23.cloned.1.call-done = bf16[2048,3072]{1,0:T(8,128)(2,1)} async-done(((bf16[256,3072]{1,0:T(8,128)(2,1)}), bf16[2048,3072]{1,0:T(8,128)(2,1)}) %all-gather.23.cloned.1.call-update) | async-done | bytes 12582928 | tf_op jit(solution)/shard_map/all_gather | solution.py:125
  803.1 11.6 %multiply_bitcast_fusion = f32[384,3072]{0,1:T(8,128)} fusion(bf16[2048,3072]{1,0:T(8,128)(2,1)} %all-gather.23.cloned.1.call-done, bf16[2048,384]{1,0:T(8,128)(2,1)} %bitcast.236), kind=kOutput, calls=%fused_computation.4 | convolution fusion | flops 4833017856 | bytes 18874368 | tf_op jit(solution)/shard_map/dot_general | solution.py:41
  814.6 6.4 copy.119
  821.0 56.1 %all-gather.21.cloned.1.call-done = bf16[2048,3072]{1,0:T(8,128)(2,1)} async-done(((bf16[256,3072]{1,0:T(8,128)(2,1)}), bf16[2048,3072]{1,0:T(8,128)(2,1)}) %all-gather.21.cloned.1.call-update) | async-done | bytes 12582928 | tf_op jit(solution)/shard_map/all_gather | solution.py:125
  877.1 11.0 %convolution_multiply_fusion = f32[384,3072]{1,0:T(8,128)} fusion(bf16[2048,384]{1,0:T(8,128)(2,1)S(1)} %bitcast.219, bf16[2048,3072]{1,0:T(8,128)(2,1)} %all-gather.21.cloned.1.call-done), kind=kOutput, calls=%fused_computation.7 | convolution fusion | flops 4833017856 | bytes 18874368 | tf_op jit(solution)/shard_map/dot_general | solution.py:41
  (150 shorter events, 53.2 us)
Async XLA Ops:
  7.2 37.8 %all-gather.9.cloned.1.call-start = ((), (), s32[]{:S(2)}) async-start(), calls=%async_computation.18 | async-start | bytes 3538944 | tf_op jit(solution)/shard_map/all_gather | solution.py:96
  7.9 2.7 copy-start.16
  7.9 144.1 %all-gather.11.cloned.1.call-start = ((), (), s32[]{:S(2)}) async-start(), calls=%async_computation.19 | async-start | bytes 10616832 | tf_op jit(solution)/shard_map/all_gather | solution.py:96
  8.7 175.2 %all-gather.13.cloned.1.call-start = ((), (), s32[]{:S(2)}) async-start(), calls=%async_computation.20 | async-start | bytes 3538944 | tf_op jit(solution)/shard_map/all_gather | solution.py:96
  9.4 277.3 %all-gather.15.cloned.1.call-start = ((), (), s32[]{:S(2)}) async-start(), calls=%async_computation.21 | async-start | bytes 21233664 | tf_op jit(solution)/shard_map/all_gather | solution.py:96
  10.0 335.2 %all-gather.17.cloned.1.call-start = ((), (), s32[]{:S(2)}) async-start(), calls=%async_computation.22 | async-start | bytes 21233664 | tf_op jit(solution)/shard_map/all_gather | solution.py:96
  10.8 2.2 copy-start.14
  10.9 2.2 copy-start.22
  10.9 2.2 copy-start.24
  12.3 35.5 %copy-start.29 = (f32[4,256]{1,0:T(4,128)}, f32[4,256]{1,0:T(4,128)S(1)}, u32[]{:S(2)}) copy-start(f32[4,256]{1,0:T(4,128)S(1)} %get-tuple-element.54) | copy-start | bytes 12292
  13.1 34.8 %copy-start.18 = (bf16[4,256,128]{1,2,0:T(8,128)(2,1)}, bf16[4,256,128]{1,2,0:T(8,128)(2,1)S(1)}, u32[]{:S(2)}) copy-start(bf16[4,256,128]{1,2,0:T(8,128)(2,1)S(1)} %convolution_convert_fusion.15) | copy-start | bytes 786436
  48.0 42.2 %copy-start.11 = (bf16[1,256,768]{2,1,0:T(8,128)(2,1)S(1)}, bf16[1,256,768]{2,1,0:T(8,128)(2,1)}, u32[]{:S(2)}) copy-start(bf16[1,256,768]{2,1,0:T(8,128)(2,1)} %param.8) | copy-start | bytes 1179652
  90.1 15.8 %copy-start.5 = (f32[256,768]{1,0:T(8,128)}, f32[256,768]{1,0:T(8,128)S(1)}, u32[]{:S(2)}) copy-start(f32[256,768]{1,0:T(8,128)S(1)} %convert_reduce_fusion.2) | copy-start | bytes 2359300
  144.4 1.1 copy-start.1
  179.6 11.2 %all-to-all-start.3 = ((bf16[8,1,32,512]{3,2,1,0:T(8,128)(2,1)}), bf16[8,1,32,512]{3,2,1,0:T(8,128)(2,1)}, u32[]{:S(2)}, u32[]{:S(2)}) async-start(bf16[8,1,32,512]{3,2,1,0:T(8,128)(2,1)} %bitcast.243), calls=%async_computation.3 | async-start | bytes 524288 | tf_op jit(solution)/shard_map/all_to_all | solution.py:135
  194.7 40.5 %copy-start.6 = (f32[256,768]{1,0:T(8,128)S(1)}, f32[256,768]{1,0:T(8,128)}, u32[]{:S(2)}) copy-start(f32[256,768]{1,0:T(8,128)} %copy-done.5) | copy-start | bytes 2359300
  234.3 0.9 copy-start.8
  276.3 1.1 copy-start.2
  357.1 10.7 %copy-start.4 = (f32[256,3072]{1,0:T(8,128)S(1)}, f32[256,3072]{1,0:T(8,128)}, u32[]{:S(2)}) copy-start(f32[256,3072]{1,0:T(8,128)} %copy.131) | copy-start | bytes 9437188
  370.4 42.5 %all-to-all-start.6 = ((bf16[256,4,768]{2,0,1:T(8,128)(2,1)}), bf16[256,4,768]{2,0,1:T(8,128)(2,1)}, u32[]{:S(2)}, u32[]{:S(2)}) async-start(bf16[256,4,768]{2,0,1:T(8,128)(2,1)} %bitcast.220), calls=%async_computation.7 | async-start | bytes 3145728 | tf_op jit(solution)/shard_map/all_to_all | solution.py:106
  418.8 41.0 %all-to-all-start.7 = ((bf16[4,256,768]{1,2,0:T(8,128)(2,1)}), bf16[4,256,768]{1,2,0:T(8,128)(2,1)}, u32[]{:S(2)}, u32[]{:S(2)}) async-start(bf16[4,256,768]{1,2,0:T(8,128)(2,1)} %broadcast_in_dim.82), calls=%async_computation.8 | async-start | bytes 3145728 | tf_op jit(solution)/shard_map/all_to_all | solution.py:101
  463.9 14.5 %all-to-all-start.8 = ((bf16[8,1,32,512]{3,2,1,0:T(8,128)(2,1)}), bf16[8,1,32,512]{3,2,1,0:T(8,128)(2,1)}, u32[]{:S(2)}, u32[]{:S(2)}) async-start(bf16[8,1,32,512]{3,2,1,0:T(8,128)(2,1)} %bitcast.255), calls=%async_computation.9 | async-start | bytes 524288 | tf_op jit(solution)/shard_map/all_to_all | solution.py:135
  467.9 238.9 %reduce-scatter.4.cloned.1.call-start = ((), (), s32[]{:S(2)}) async-start(), calls=%async_computation.23 | async-start | bytes 1966080 | tf_op jit(solution)/shard_map/reduce_scatter | solution.py:115
  480.1 4.3 copy-start.17
  480.1 4.3 copy-start.20
  480.1 4.3 copy-start.28
  481.4 3.3 copy-start.21
  490.0 7.9 copy-start.3
  500.4 45.5 %all-to-all-start.9 = ((bf16[256,4,768]{2,0,1:T(8,128)(2,1)}), bf16[256,4,768]{2,0,1:T(8,128)(2,1)}, u32[]{:S(2)}, u32[]{:S(2)}) async-start(bf16[256,4,768]{2,0,1:T(8,128)(2,1)} %bitcast.221), calls=%async_computation.10 | async-start | bytes 3145728 | tf_op jit(solution)/shard_map/all_to_all | solution.py:106
  504.8 204.0 %reduce-scatter.8.cloned.1.call-start = ((), (), s32[]{:S(2)}) async-start(), calls=%async_computation.26 | async-start | bytes 3538944 | tf_op jit(solution)/shard_map/reduce_scatter | solution.py:129
  508.8 213.7 %reduce-scatter.6.cloned.1.call-start = ((), (), s32[]{:S(2)}) async-start(), calls=%async_computation.24 | async-start | bytes 3538944 | tf_op jit(solution)/shard_map/reduce_scatter | solution.py:129
  563.7 42.1 %copy-start.19 = (bf16[4,256,128]{1,2,0:T(8,128)(2,1)S(1)}, bf16[4,256,128]{1,2,0:T(8,128)(2,1)}, u32[]{:S(2)}) copy-start(bf16[4,256,128]{1,2,0:T(8,128)(2,1)} %copy-done.18) | copy-start | bytes 786436
  604.6 1.1 copy-start.13
  608.5 120.7 %all-gather.19.cloned.1.call-start = ((), (), s32[]{:S(2)}) async-start(), calls=%async_computation.25 | async-start | bytes 7077888 | tf_op jit(solution)/shard_map/all_gather | solution.py:125
  609.2 193.8 %all-gather.23.cloned.1.call-start = ((), (), s32[]{:S(2)}) async-start(), calls=%async_computation.28 | async-start | bytes 14155776 | tf_op jit(solution)/shard_map/all_gather | solution.py:125
  609.8 267.3 %all-gather.21.cloned.1.call-start = ((), (), s32[]{:S(2)}) async-start(), calls=%async_computation.27 | async-start | bytes 14155776 | tf_op jit(solution)/shard_map/all_gather | solution.py:125
  613.3 33.4 %all-to-all-start.14 = ((bf16[256,8,384]{0,2,1:T(8,128)(2,1)}), bf16[256,8,384]{0,2,1:T(8,128)(2,1)}, u32[]{:S(2)}, u32[]{:S(2)}) async-start(bf16[256,8,384]{0,2,1:T(8,128)(2,1)} %bitcast.222), calls=%async_computation.17 | async-start | bytes 3145728 | tf_op jit(solution)/shard_map/all_to_all | solution.py:121
  619.1 31.9 %copy-start = (f32[4,256,768]{1,2,0:T(8,128)S(1)}, f32[4,256,768]{1,2,0:T(8,128)}, u32[]{:S(2)}) copy-start(f32[4,256,768]{1,2,0:T(8,128)} %convert_element_type.340) | copy-start | bytes 9437188
  646.7 28.2 %all-to-all-start.12 = ((bf16[256,8,384]{0,2,1:T(8,128)(2,1)}), bf16[256,8,384]{0,2,1:T(8,128)(2,1)}, u32[]{:S(2)}, u32[]{:S(2)}) async-start(bf16[256,8,384]{0,2,1:T(8,128)(2,1)} %multiply_convert_fusion.3), calls=%async_computation.14 | async-start | bytes 3145728 | tf_op jit(solution)/shard_map/all_to_all | solution.py:121
  651.0 28.2 %copy-start.30 = (f32[4,256]{1,0:T(4,128)S(1)}, f32[4,256]{1,0:T(4,128)}, u32[]{:S(2)}) copy-start(f32[4,256]{1,0:T(4,128)} %copy-done.29) | copy-start | bytes 12292
  674.8 29.4 %all-to-all-start.13 = ((bf16[256,8,384]{0,2,1:T(8,128)(2,1)}), bf16[256,8,384]{0,2,1:T(8,128)(2,1)}, u32[]{:S(2)}, u32[]{:S(2)}) async-start(bf16[256,8,384]{0,2,1:T(8,128)(2,1)} %multiply_convert_fusion.2), calls=%async_computation.16 | async-start | bytes 3145728 | tf_op jit(solution)/shard_map/all_to_all | solution.py:121
  681.8 25.1 %copy-start.7 = (f32[256,768]{1,0:T(8,128)S(1)}, f32[256,768]{1,0:T(8,128)}, u32[]{:S(2)}) copy-start(f32[256,768]{1,0:T(8,128)} %copy-done.5) | copy-start | bytes 2359300
  681.8 25.1 %copy-start.9 = (f32[256,768]{1,0:T(8,128)S(1)}, f32[256,768]{1,0:T(8,128)}, u32[]{:S(2)}) copy-start(f32[256,768]{1,0:T(8,128)} %copy-done.8) | copy-start | bytes 2359300
  681.8 25.1 %copy-start.12 = (bf16[1,256,768]{2,1,0:T(8,128)(2,1)S(1)}, bf16[1,256,768]{2,1,0:T(8,128)(2,1)}, u32[]{:S(2)}) copy-start(bf16[1,256,768]{2,1,0:T(8,128)(2,1)} %param.8) | copy-start | bytes 1179652
  710.7 3.5 copy-start.15
  710.7 5.1 copy-start.23
  710.7 5.1 copy-start.25
  718.9 1.4 copy-start.26
  718.9 1.4 copy-start.27
  814.6 62.5 %copy-start.10 = (bf16[8,256,384]{2,1,0:T(8,128)(2,1)S(1)}, bf16[8,256,384]{2,1,0:T(8,128)(2,1)}, u32[]{:S(2)}) copy-start(bf16[8,256,384]{2,1,0:T(8,128)(2,1)} %copy.115) | copy-start | bytes 4718596
Sparse Core Ops, SparseCore 0:
  9.9 35.0 all-gather.8
  46.8 63.0 all-gather.10
  111.8 32.3 all-gather.12
  145.9 98.7 all-gather.14
  246.4 98.7 all-gather.16
  478.5 37.0 reduce-scatter.3
  519.0 55.7 reduce-scatter.7
  608.6 52.4 reduce-scatter.5
  663.0 66.1 all-gather.18
  730.9 72.1 all-gather.22
  805.0 72.1 all-gather.20

commit v2 on v1

--- a/solution.py
+++ b/solution.py
@@ -163,6 +163,10 @@
     spot_count = patches // devices
     row_count = local_frames * patches
     spatial_output, spatial_back = jax.vjp(spatial, spatial_qkv)
+    upstream_rows = upstream.reshape(row_count, upstream.shape[2])
+    spatial_output, upstream_own = lax.optimization_barrier(
+        (spatial_output, own_columns(upstream_rows))
+    )
     spatial_full = fetch_rows(spatial_out)
     first_mid = (
         latents.reshape(row_count, narrow).astype(jnp.float32)
@@ -191,7 +195,10 @@
     block_out = (second_mid.astype(jnp.float32) + late_sum(times_t(hidden_act, outer_full))).astype(
         jnp.bfloat16
     )
-    upstream_rows = upstream.reshape(row_count, upstream.shape[2])
+    upstream_rows, first_own, second_own = lax.optimization_barrier(
+        (upstream_rows, own_columns(first_norm), own_columns(second_norm))
+    )
+    hidden_all = all_tokens(hidden_act)
     upstream_cols = lax.dynamic_slice_in_dim(
         upstream_rows, lax.axis_index("fsdp") * narrow, narrow, 1
     )
@@ -201,7 +208,8 @@
         upstream_cols.astype(jnp.float32)
         + head_sum(norm_back(second_wide, times_t(pre_grad, inner_full)))
     ).astype(jnp.bfloat16)
-    second_grad_wide = widen(second_grad)
+    pre_all = all_tokens(pre_grad)
+    second_grad_wide, hidden_all = lax.optimization_barrier((widen(second_grad), hidden_all))
     temporal_grad = to_positions(
         jnp.dot(second_grad_wide, out_full, preferred_element_type=jnp.float32).astype(
             jnp.bfloat16
@@ -209,23 +217,27 @@
         local_frames,
     )
     triple_grad = temporal_back(temporal_grad)[0]
-    first_back = head_sum(norm_back(first_wide, times_t(triple_grad, triple_full))).astype(
-        jnp.bfloat16
-    )
+    triple_grad, spatial_late = lax.optimization_barrier((triple_grad, spatial_output))
+    triple_all = all_tokens(triple_grad)
+    spatial_all = all_tokens(spatial_late)
+    back_terms, pre_all = lax.optimization_barrier(
+        (norm_back(first_wide, times_t(triple_grad, triple_full)).astype(jnp.bfloat16), pre_all)
+    )
+    first_back = head_sum(back_terms).astype(jnp.bfloat16)
     first_grad = (
         second_grad.astype(jnp.float32) + to_frames(first_back, local_frames).astype(jnp.float32)
     ).astype(jnp.bfloat16)
-    first_grad_wide = widen(first_grad)
+    first_grad_wide, triple_all = lax.optimization_barrier((widen(first_grad), triple_all))
     spatial_grad = jnp.dot(
         first_grad_wide, spatial_full, preferred_element_type=jnp.float32
     ).astype(jnp.bfloat16)
     grad_spatial_qkv = spatial_back(spatial_grad)[0]
     grads = (
-        send_rows(left_times(first_grad_wide, spatial_output)),
-        left_times(own_columns(first_norm), all_tokens(triple_grad)),
+        left_times(own_columns(first_grad_wide), spatial_all),
+        left_times(first_own, triple_all),
         send_rows(left_times(second_grad_wide, frames_result)),
-        left_times(own_columns(second_norm), all_tokens(pre_grad)),
-        left_times(own_columns(upstream_rows), all_tokens(hidden_act)),
+        left_times(second_own, pre_all),
+        left_times(upstream_own, hidden_all),
     )
     return (
         block_out.reshape(local_frames, patches, narrow),

time: 905 us -> 761 us (0.84)
  waiting for transfers between devices: 395 us -> 262 us
  blocking collectives: 228 us -> 243 us
  matrix products: 133 us -> 120 us
  local copies, waits for them, and re-layouts: 57.6 us -> 47.7 us
    all_to_all x2 -> x3, blocking collectives: 81.2 us -> 150 us  [head_sum(): lax.all_to_all(terms.astype(jnp.bfloat16), 'fsdp', split_axis=1, concat_a...]
    all_gather x5, waiting for transfers between devices: 74.8 us -> 8.81 us  [fetch_rows(): return lax.all_gather(weight, 'seq', axis=0, tiled=True)]
    all_gather x3 -> x4, waiting for transfers between devices: 128 us -> 72 us  [all_tokens(): return lax.all_gather(table, 'seq', axis=0, tiled=True)]
    all_to_all x2 -> x1, waiting for transfers between devices: 74.5 us -> 26.9 us  [head_sum(): lax.all_to_all(terms.astype(jnp.bfloat16), 'fsdp', split_axis=1, concat_a...]
    all_to_all x3 -> x2, blocking collectives: 118 us -> 78.2 us  [widen(): lax.all_to_all(copies, 'fsdp', split_axis=0, concat_axis=2, tiled=True)[0]]
    all_to_all x2 -> x3, waiting for transfers between devices: 6.93 us -> 22.2 us  [regroup(): return lax.all_to_all(block, 'seq', split_axis=0, concat_axis=1, tiled=True)]
    all_to_all x2 -> x1, blocking collectives: 28.6 us -> 15.3 us  [regroup(): return lax.all_to_all(block, 'seq', split_axis=0, concat_axis=1, tiled=True)]
    all_to_all x3 -> x4, waiting for transfers between devices: 70.4 us -> 82.7 us  [own_columns(): return lax.all_to_all(table, 'seq', split_axis=1, concat_axis=0, tiled=True)]
  transfers between devices with their start and end apart: 19 -> 21, of which waited for: 12 -> 15; matrix products, arithmetic and copies ran while one was open for 19% -> 23% of each run, Pallas kernels for 0% -> 0%
where the time goes in v2:
time: 761 us; the launch traced here: 756 us
  waiting for transfers between devices  262 us (34%)
  blocking collectives  243 us (32%)
  matrix products  120 us (16%)
  local copies, waits for them, and re-layouts  47.7 us (6%)
  starting transfers between devices  42.1 us (6%)
  other arithmetic  25.1 us (3%)
  between operations  15.2 us (2%)
    all_to_all x3, blocking collectives, head_sum(): lax.all_to_all(terms.astype(jnp.bfloat16), 'fsdp', split_axis=1, concat_a...  150 us
    all_to_all x4, waiting for transfers between devices, own_columns(): return lax.all_to_all(table, 'seq', split_axis=1, concat_axis=0, tiled=True)  82.7 us
    all_to_all x2, blocking collectives, widen(): lax.all_to_all(copies, 'fsdp', split_axis=0, concat_axis=2, tiled=True)[0]  78.2 us
    all_gather x4, waiting for transfers between devices, all_tokens(): return lax.all_gather(table, 'seq', axis=0, tiled=True)  72 us
    all_to_all x2, waiting for transfers between devices, widen(): lax.all_to_all(copies, 'fsdp', split_axis=0, concat_axis=2, tiled=True)[0]  41.1 us
    dot_general x5, matrix products, left_times(): lax.dot_general(matrix, factor, (((0,), (0,)), ((), ())), preferred_eleme...  36.7 us
    dot_general x5, matrix products, times_t(): lax.dot_general(matrix, factor, (((1,), (1,)), ((), ())), preferred_eleme...  33 us
    all_to_all x1, waiting for transfers between devices, head_sum(): lax.all_to_all(terms.astype(jnp.bfloat16), 'fsdp', split_axis=1, concat_a...  26.9 us
  transfers between devices with their start and end apart: 21, of which 15 were waited for; matrix products, arithmetic and copies ran while one was open for 23% of the time, Pallas kernels for 0%

profile of v2, /device:TPU:0, one launch (start us, length us, event | category | flops | bytes accessed | tf_op | source)
XLA Modules:
  0.0 755.7 jit_solution(16230801153515134060)
XLA Ops:
  12.1 5.2 all-to-all-start
  19.9 22.6 %all-to-all-done = bf16[256,8,384]{0,2,1:T(8,128)(2,1)S(1)} async-done(((bf16[256,8,384]{0,2,1:T(8,128)(2,1)}), bf16[256,8,384]{0,2,1:T(8,128)(2,1)S(1)}, u32[]{:S(2)}, u32[]{:S(2)}) %all-to-all-start) | async-done | bytes 1572896 | tf_op jit(solution)/shard_map/all_to_all | solution.py:121
  44.1 8.5 %all-gather.10.cloned.1.call-done = bf16[3072,512]{1,0:T(8,128)(2,1)} async-done(((bf16[384,512]{1,0:T(8,128)(2,1)}), bf16[3072,512]{1,0:T(8,128)(2,1)}) %all-gather.10.cloned.1.call-update) | async-done | bytes 3145744 | tf_op jit(solution)/shard_map/all_gather | solution.py:96
  52.6 2.9 convolution_convert_fusion.2
  55.7 42.2 %all_to_all.206 = bf16[256,4,768]{2,0,1:T(8,128)(2,1)S(1)} all-to-all(bf16[256,4,768]{2,0,1:T(8,128)(2,1)S(1)} %bitcast.221), channel_id=1, replica_groups=mesh['seq'=8,'fsdp'=4] {'fsdp'}, dimensions={1} | all-to-all | bytes 3145728 | tf_op jit(solution)/shard_map/all_to_all | solution.py:106
  99.1 15.3 %all_to_all.207 = bf16[8,1,32,768]{3,2,1,0:T(8,128)(2,1)S(1)} all-to-all(bf16[8,1,32,768]{3,2,1,0:T(8,128)(2,1)S(1)} %add_convert_fusion.3), channel_id=1, replica_groups=mesh['seq'=8,'fsdp'=4] {'seq'}, dimensions={0} | all-to-all | bytes 786432 | tf_op jit(solution)/shard_map/all_to_all | solution.py:135
  114.6 39.0 %all_to_all.208 = bf16[4,256,768]{1,2,0:T(8,128)(2,1)S(1)} all-to-all(bf16[4,256,768]{1,2,0:T(8,128)(2,1)S(1)} %broadcast_in_dim.33), channel_id=1, replica_groups=mesh['seq'=8,'fsdp'=4] {'fsdp'}, dimensions={0} | all-to-all | bytes 3145728 | tf_op jit(solution)/shard_map/all_to_all | solution.py:101
  155.1 2.4 copy.129
  157.4 1.8 convert_reduce_fusion.4
  159.3 2.2 fusion.12
  161.5 9.6 %convolution_convert_fusion.3 = bf16[256,1536]{1,0:T(8,128)(2,1)} fusion(bf16[3072,1536]{1,0:T(8,128)(2,1)} %all-gather.12.cloned.1.call-done, f32[256,3072]{1,0:T(8,128)} %copy.129, f32[256]{0:T(256)S(1)} %add_rsqrt_fusion.1, f32[256]{0:T(256)S(1)} %broadcast_multiply_fusion.5), kind=kOutput, calls=%fused_computation.36 | convolution fusion | flops 2418671616 | bytes 13371392 | tf_op jit(solution)/shard_map/dot_general | solution.py:178
  171.0 3.6 reshape.287
  174.6 3.7 fusion.56
  181.4 3.0 fusion.60
  186.6 1.8 reshape.289
  188.4 4.1 all-to-all-start.4
  192.5 6.9 all-to-all-done.4
  199.4 3.0 convolution_convert_fusion.1
  202.5 40.3 %all_to_all.209 = bf16[256,4,768]{2,0,1:T(8,128)(2,1)S(1)} all-to-all(bf16[256,4,768]{2,0,1:T(8,128)(2,1)S(1)} %bitcast.222), channel_id=1, replica_groups=mesh['seq'=8,'fsdp'=4] {'fsdp'}, dimensions={1} | all-to-all | bytes 3145728 | tf_op jit(solution)/shard_map/all_to_all | solution.py:106
  247.2 4.4 all-to-all-start.6
  253.1 34.6 %all-to-all-done.6 = bf16[4,256,768]{1,2,0:T(8,128)(2,1)} async-done(((bf16[4,256,768]{1,2,0:T(8,128)(2,1)}), bf16[4,256,768]{1,2,0:T(8,128)(2,1)}, u32[]{:S(2)}, u32[]{:S(2)}) %all-to-all-start.6) | async-done | bytes 1572896 | tf_op jit(solution)/shard_map/all_to_all | solution.py:101
  287.7 4.3 all-to-all-start.7
  292.0 1.7 convert_element_type.319
  293.7 1.8 convert_reduce_fusion.3
  295.5 1.9 fusion.10
  298.9 26.9 %all-to-all-done.7 = bf16[256,8,384]{0,2,1:T(8,128)(2,1)} async-done(((bf16[256,8,384]{0,2,1:T(8,128)(2,1)}), bf16[256,8,384]{0,2,1:T(8,128)(2,1)}, u32[]{:S(2)}, u32[]{:S(2)}) %all-to-all-start.7) | async-done | bytes 1572896 | tf_op jit(solution)/shard_map/all_to_all | solution.py:121
  325.8 4.5 all-to-all-start.8
  330.3 2.7 copy.100
  333.0 2.3 copy.130
  335.3 33.1 %all-to-all-done.8 = bf16[256,8,384]{0,2,1:T(8,128)(2,1)} async-done(((bf16[256,8,384]{0,2,1:T(8,128)(2,1)}), bf16[256,8,384]{0,2,1:T(8,128)(2,1)}, u32[]{:S(2)}, u32[]{:S(2)}) %all-to-all-start.8) | async-done | bytes 1572896 | tf_op jit(solution)/shard_map/all_to_all | solution.py:121
  368.4 2.6 copy.101
  371.0 10.8 %fusion.61 = f32[256,3072]{1,0:T(8,128)} fusion(bf16[256,3072]{1,0:T(8,128)(2,1)} %bitcast.230, bf16[3072,3072]{1,0:T(8,128)(2,1)} %all-gather.18.cloned.1.call-done), kind=kOutput, calls=%fused_computation.131 | convolution fusion | flops 4831838208 | bytes 23592960 | tf_op jit(solution)/shard_map/dot_general | solution.py:205
  382.1 12.4 %fusion.8 = (bf16[256,3072]{1,0:T(8,128)(2,1)}, bf16[256,3072]{1,0:T(8,128)(2,1)}) fusion(f32[256,3072]{1,0:T(8,128)} %fusion.61, bf16[3072,3072]{1,0:T(8,128)(2,1)} %all-gather.16.cloned.1.call-done, f32[256,3072]{1,0:T(8,128)S(1)} %copy-done.2, f32[256]{0:T(256)S(1)} %add_rsqrt_fusion, f32[256]{0:T(256)S(1)} %broadcast_multiply_fusion.4), kind=kOutput, calls=%fused_computation.16 | convolution fusion | flops 4851499008 | bytes 28313600 | tf_op jit(solution)/shard_map/dot_general | solution.py:192
  395.3 10.9 %fusion.55 = (f32[256]{0:T(256)S(1)}, f32[256]{0:T(256)S(1)}, f32[256,3072]{1,0:T(8,128)S(1)}) fusion(f32[256]{0:T(256)S(1)} %add_rsqrt_fusion, f32[256,3072]{1,0:T(8,128)S(1)} %copy-done.2, f32[256]{0:T(256)S(1)} %broadcast_multiply_fusion.4, bf16[256,3072]{1,0:T(8,128)(2,1)} %get-tuple-element.70, bf16[3072,3072]{1,0:T(8,128)(2,1)} %all-gather.16.cloned.1.call-done), kind=kOutput, calls=%fused_computation.125 | convolution fusion | flops 4835770368 | bytes 26742784 | tf_op jit(solution)/shard_map/dot_general | solution.py:34
  408.7 3.6 all-to-all-start.9
  412.6 10.3 %convolution_convert_fusion = bf16[256,3072]{1,0:T(8,128)(2,1)} fusion(bf16[256,3072]{1,0:T(8,128)(2,1)S(1)} %copy-done.14, bf16[3072,3072]{1,0:T(8,128)(2,1)} %all-gather.18.cloned.1.call-done), kind=kOutput, calls=%fused_computation.7 | convolution fusion | flops 4832624640 | bytes 22020096 | tf_op jit(solution)/shard_map/dot_general | solution.py:34
  423.0 26.9 %all-to-all-done.9 = bf16[256,4,768]{2,0,1:T(8,128)(2,1)S(1)} async-done(((bf16[256,4,768]{2,0,1:T(8,128)(2,1)}), bf16[256,4,768]{2,0,1:T(8,128)(2,1)S(1)}, u32[]{:S(2)}, u32[]{:S(2)}) %all-to-all-start.9) | async-done | bytes 1572896 | tf_op jit(solution)/shard_map/all_to_all | solution.py:106
  451.4 39.2 %all_to_all.210 = bf16[4,256,768]{1,2,0:T(8,128)(2,1)S(1)} all-to-all(bf16[4,256,768]{1,2,0:T(8,128)(2,1)S(1)} %broadcast_in_dim.36), channel_id=1, replica_groups=mesh['seq'=8,'fsdp'=4] {'fsdp'}, dimensions={0} | all-to-all | bytes 3145728 | tf_op jit(solution)/shard_map/all_to_all | solution.py:101
  491.8 3.6 multiply_convert_fusion
  495.5 1.9 copy-done.12
  497.4 3.1 convolution_convert_fusion.13
  500.5 3.6 all-to-all-start.11
  505.0 9.1 %all-to-all-done.11 = bf16[8,1,32,512]{3,2,1,0:T(8,128)(2,1)S(1)} async-done(((bf16[8,1,32,512]{3,2,1,0:T(8,128)(2,1)}), bf16[8,1,32,512]{3,2,1,0:T(8,128)(2,1)S(1)}, u32[]{:S(2)}, u32[]{:S(2)}) %all-to-all-start.11) | async-done | bytes 262176 | tf_op jit(solution)/shard_map/all_to_all | solution.py:135
  517.0 1.7 copy.157
  518.7 3.2 reshape.294
  521.9 5.8 fusion.54
  527.7 2.3 multiply_convert_fusion.1
  530.1 12.3 %all-gather.22.cloned.1.call-done = bf16[2048,3072]{1,0:T(8,128)(2,1)} async-done(((bf16[256,3072]{1,0:T(8,128)(2,1)}), bf16[2048,3072]{1,0:T(8,128)(2,1)}) %all-gather.22.cloned.1.call-update) | async-done | bytes 12582928 | tf_op jit(solution)/shard_map/all_gather | solution.py:125
  543.9 67.2 %all_to_all.211 = bf16[256,4,768]{2,0,1:T(8,128)(2,1)S(1)} all-to-all(bf16[256,4,768]{2,0,1:T(8,128)(2,1)S(1)} %bitcast.223), channel_id=1, replica_groups=mesh['seq'=8,'fsdp'=4] {'fsdp'}, dimensions={1} | all-to-all | bytes 3145728 | tf_op jit(solution)/shard_map/all_to_all | solution.py:106
  612.2 3.5 all-to-all-start.13
  615.7 2.0 fusion.42
  617.8 6.1 all-to-all-done.13
  625.5 3.8 all-to-all-start.14
  629.3 11.3 %convolution_multiply_fusion = f32[384,3072]{1,0:T(8,128)} fusion(bf16[2048,384]{1,0:T(8,128)(2,1)S(1)} %bitcast.214, bf16[2048,3072]{1,0:T(8,128)(2,1)} %all-gather.20.cloned.1.call-done), kind=kOutput, calls=%fused_computation.5 | convolution fusion | flops 4833017856 | bytes 18874368 | tf_op jit(solution)/shard_map/dot_general | solution.py:41
  640.6 10.9 %convolution_multiply_fusion.1 = f32[384,3072]{1,0:T(8,128)} fusion(bf16[2048,384]{1,0:T(8,128)(2,1)S(1)} %bitcast.215, bf16[2048,3072]{1,0:T(8,128)(2,1)} %all-gather.22.cloned.1.call-done), kind=kOutput, calls=%fused_computation.6 | convolution fusion | flops 4833017856 | bytes 18874368 | tf_op jit(solution)/shard_map/dot_general | solution.py:41
  651.5 4.8 reduce-scatter.5.cloned.1.call-done
  656.4 2.0 convert_element_type.306
  658.3 6.5 all-to-all-done.14
  664.8 39.5 %all-gather.24.cloned.1.call-done = bf16[2048,1536]{1,0:T(8,128)(2,1)} async-done(((bf16[256,1536]{1,0:T(8,128)(2,1)}), bf16[2048,1536]{1,0:T(8,128)(2,1)}) %all-gather.24.cloned.1.call-update) | async-done | bytes 6291472 | tf_op jit(solution)/shard_map/all_gather | solution.py:125
  704.4 2.9 convolution_convert_fusion.8
  709.0 4.7 all-to-all-start.15
  717.8 6.8 convolution_multiply_fusion.2
  724.6 20.1 %all-gather.26.cloned.1.call-done = bf16[2048,512]{0,1:T(8,128)(2,1)} async-done(((bf16[256,512]{0,1:T(8,128)(2,1)}), bf16[2048,512]{0,1:T(8,128)(2,1)}) %all-gather.26.cloned.1.call-update) | async-done | bytes 2097168 | tf_op jit(solution)/shard_map/all_gather | solution.py:125
  744.7 4.0 convolution_multiply_fusion.4
  (150 shorter events, 45.0 us)
Async XLA Ops:
  7.2 45.4 %all-gather.10.cloned.1.call-start = ((), (), s32[]{:S(2)}) async-start(), calls=%async_computation.18 | async-start | bytes 3538944 | tf_op jit(solution)/shard_map/all_gather | solution.py:96
  7.9 2.7 copy-start.13
  7.9 153.5 %all-gather.12.cloned.1.call-start = ((), (), s32[]{:S(2)}) async-start(), calls=%async_computation.19 | async-start | bytes 10616832 | tf_op jit(solution)/shard_map/all_gather | solution.py:96
  8.7 183.8 %all-gather.14.cloned.1.call-start = ((), (), s32[]{:S(2)}) async-start(), calls=%async_computation.20 | async-start | bytes 3538944 | tf_op jit(solution)/shard_map/all_gather | solution.py:96
  9.4 361.6 %all-gather.18.cloned.1.call-start = ((), (), s32[]{:S(2)}) async-start(), calls=%async_computation.22 | async-start | bytes 21233664 | tf_op jit(solution)/shard_map/all_gather | solution.py:96
  10.0 372.1 %all-gather.16.cloned.1.call-start = ((), (), s32[]{:S(2)}) async-start(), calls=%async_computation.21 | async-start | bytes 21233664 | tf_op jit(solution)/shard_map/all_gather | solution.py:96
  10.6 6.8 copy-start.21
  12.1 30.4 %all-to-all-start = ((bf16[256,8,384]{0,2,1:T(8,128)(2,1)}), bf16[256,8,384]{0,2,1:T(8,128)(2,1)S(1)}, u32[]{:S(2)}, u32[]{:S(2)}) async-start(bf16[256,8,384]{0,2,1:T(8,128)(2,1)} %bitcast.7), calls=%async_computation | async-start | bytes 3145728 | tf_op jit(solution)/shard_map/all_to_all | solution.py:121
  17.6 2.2 copy-start.19
  17.6 2.2 copy-start.25
  17.6 2.2 copy-start.27
  19.9 35.7 %copy-start.17 = (bf16[4,256,128]{1,2,0:T(8,128)(2,1)}, bf16[4,256,128]{1,2,0:T(8,128)(2,1)S(1)}, u32[]{:S(2)}) copy-start(bf16[4,256,128]{1,2,0:T(8,128)(2,1)S(1)} %convolution_convert_fusion.15) | copy-start | bytes 786436
  55.7 43.3 %copy-start.11 = (bf16[1,256,768]{2,1,0:T(8,128)(2,1)S(1)}, bf16[1,256,768]{2,1,0:T(8,128)(2,1)}, u32[]{:S(2)}) copy-start(bf16[1,256,768]{2,1,0:T(8,128)(2,1)} %param.8) | copy-start | bytes 1179652
  98.1 0.9 copy-start.3
  153.6 1.1 copy-start
  188.4 11.0 %all-to-all-start.4 = ((bf16[8,1,32,512]{3,2,1,0:T(8,128)(2,1)}), bf16[8,1,32,512]{3,2,1,0:T(8,128)(2,1)}, u32[]{:S(2)}, u32[]{:S(2)}) async-start(bf16[8,1,32,512]{3,2,1,0:T(8,128)(2,1)} %bitcast.241), calls=%async_computation.4 | async-start | bytes 524288 | tf_op jit(solution)/shard_map/all_to_all | solution.py:135
  202.5 41.4 %copy-start.4 = (f32[256,768]{1,0:T(8,128)S(1)}, f32[256,768]{1,0:T(8,128)}, u32[]{:S(2)}) copy-start(f32[256,768]{1,0:T(8,128)} %copy-done.3) | copy-start | bytes 2359300
  243.1 0.9 copy-start.7
  247.2 40.5 %all-to-all-start.6 = ((bf16[4,256,768]{1,2,0:T(8,128)(2,1)}), bf16[4,256,768]{1,2,0:T(8,128)(2,1)}, u32[]{:S(2)}, u32[]{:S(2)}) async-start(bf16[4,256,768]{1,2,0:T(8,128)(2,1)} %broadcast_in_dim.35), calls=%async_computation.6 | async-start | bytes 3145728 | tf_op jit(solution)/shard_map/all_to_all | solution.py:101
  287.7 38.1 %all-to-all-start.7 = ((bf16[256,8,384]{0,2,1:T(8,128)(2,1)}), bf16[256,8,384]{0,2,1:T(8,128)(2,1)}, u32[]{:S(2)}, u32[]{:S(2)}) async-start(bf16[256,8,384]{0,2,1:T(8,128)(2,1)} %multiply_convert_fusion.4), calls=%async_computation.8 | async-start | bytes 3145728 | tf_op jit(solution)/shard_map/all_to_all | solution.py:121
  325.8 42.6 %all-to-all-start.8 = ((bf16[256,8,384]{0,2,1:T(8,128)(2,1)}), bf16[256,8,384]{0,2,1:T(8,128)(2,1)}, u32[]{:S(2)}, u32[]{:S(2)}) async-start(bf16[256,8,384]{0,2,1:T(8,128)(2,1)} %multiply_convert_fusion.3), calls=%async_computation.9 | async-start | bytes 3145728 | tf_op jit(solution)/shard_map/all_to_all | solution.py:121
  330.3 160.4 %all-gather.20.cloned.1.call-start = ((), (), s32[]{:S(2)}) async-start(), calls=%async_computation.24 | async-start | bytes 14155776 | tf_op jit(solution)/shard_map/all_gather | solution.py:125
  371.0 11.1 %copy-start.2 = (f32[256,3072]{1,0:T(8,128)S(1)}, f32[256,3072]{1,0:T(8,128)}, u32[]{:S(2)}) copy-start(f32[256,3072]{1,0:T(8,128)} %copy.130) | copy-start | bytes 9437188
  394.5 147.8 %all-gather.22.cloned.1.call-start = ((), (), s32[]{:S(2)}) async-start(), calls=%async_computation.25 | async-start | bytes 14155776 | tf_op jit(solution)/shard_map/all_gather | solution.py:125
  407.4 5.1 copy-start.14
  408.7 41.1 %all-to-all-start.9 = ((bf16[256,4,768]{2,0,1:T(8,128)(2,1)}), bf16[256,4,768]{2,0,1:T(8,128)(2,1)S(1)}, u32[]{:S(2)}, u32[]{:S(2)}) async-start(bf16[256,4,768]{2,0,1:T(8,128)(2,1)} %bitcast.202), calls=%async_computation.10 | async-start | bytes 3145728 | tf_op jit(solution)/shard_map/all_to_all | solution.py:106
  412.3 203.4 %reduce-scatter.3.cloned.1.call-start = ((), (), s32[]{:S(2)}) async-start(), calls=%async_computation.23 | async-start | bytes 1966080 | tf_op jit(solution)/shard_map/reduce_scatter | solution.py:115
  422.9 233.4 %reduce-scatter.5.cloned.1.call-start = ((), (), s32[]{:S(2)}) async-start(), calls=%async_computation.28 | async-start | bytes 3538944 | tf_op jit(solution)/shard_map/reduce_scatter | solution.py:129
  490.7 1.2 copy-start.15
  495.5 1.9 copy-start.12
  500.5 15.5 %copy-start.22 = (f32[128,8,8]{1,2,0:T(8,128)S(1)}, f32[128,8,8]{1,2,0:T(8,128)}, u32[]{:S(2)}) copy-start(f32[128,8,8]{1,2,0:T(8,128)} %get-tuple-element.85) | copy-start | bytes 98308
  500.5 15.5 %copy-start.29 = (f32[128,8]{1,0:T(8,128)S(1)}, f32[128,8]{1,0:T(8,128)}, u32[]{:S(2)}) copy-start(f32[128,8]{1,0:T(8,128)} %get-tuple-element.84) | copy-start | bytes 12292
  500.5 15.8 %copy-start.24 = (bf16[1,32,4,8,128]{4,3,2,1,0:T(8,128)(2,1)S(1)}, bf16[1,32,4,8,128]{4,3,2,1,0:T(8,128)(2,1)}, u32[]{:S(2)}) copy-start(bf16[1,32,4,8,128]{4,3,2,1,0:T(8,128)(2,1)} %copy.92) | copy-start | bytes 786436
  500.5 13.6 %all-to-all-start.11 = ((bf16[8,1,32,512]{3,2,1,0:T(8,128)(2,1)}), bf16[8,1,32,512]{3,2,1,0:T(8,128)(2,1)S(1)}, u32[]{:S(2)}, u32[]{:S(2)}) async-start(bf16[8,1,32,512]{3,2,1,0:T(8,128)(2,1)} %bitcast.251), calls=%async_computation.12 | async-start | bytes 524288 | tf_op jit(solution)/shard_map/all_to_all | solution.py:135
  504.0 200.3 %all-gather.24.cloned.1.call-start = ((), (), s32[]{:S(2)}) async-start(), calls=%async_computation.26 | async-start | bytes 7077888 | tf_op jit(solution)/shard_map/all_gather | solution.py:125
  514.4 2.2 copy-start.23
  516.9 5.0 copy-start.1
  543.9 71.8 %copy-start.5 = (f32[256,768]{1,0:T(8,128)S(1)}, f32[256,768]{1,0:T(8,128)}, u32[]{:S(2)}) copy-start(f32[256,768]{1,0:T(8,128)} %copy-done.3) | copy-start | bytes 2359300
  543.9 71.8 %copy-start.8 = (f32[256,768]{1,0:T(8,128)S(1)}, f32[256,768]{1,0:T(8,128)}, u32[]{:S(2)}) copy-start(f32[256,768]{1,0:T(8,128)} %copy-done.7) | copy-start | bytes 2359300
  612.2 11.7 %all-to-all-start.13 = ((bf16[8,1,32,768]{3,2,1,0:T(8,128)(2,1)}), bf16[8,1,32,768]{3,2,1,0:T(8,128)(2,1)S(1)}, u32[]{:S(2)}, u32[]{:S(2)}) async-start(bf16[8,1,32,768]{3,2,1,0:T(8,128)(2,1)} %bitcast.236), calls=%async_computation.14 | async-start | bytes 786432 | tf_op jit(solution)/shard_map/all_to_all | solution.py:135
  615.6 129.1 %all-gather.26.cloned.1.call-start = ((), (), s32[]{:S(2)}) async-start(), calls=%async_computation.27 | async-start | bytes 2359296 | tf_op jit(solution)/shard_map/all_gather | solution.py:125
  624.0 1.4 copy-start.16
  624.0 5.3 copy-start.9
  625.5 39.4 %all-to-all-start.14 = ((bf16[4,256,768]{1,2,0:T(8,128)(2,1)}), bf16[4,256,768]{1,2,0:T(8,128)(2,1)S(1)}, u32[]{:S(2)}, u32[]{:S(2)}) async-start(bf16[4,256,768]{1,2,0:T(8,128)(2,1)} %broadcast_in_dim.83), calls=%async_computation.15 | async-start | bytes 3145728 | tf_op jit(solution)/shard_map/all_to_all | solution.py:101
  629.3 11.3 %copy-start.10 = (bf16[8,256,384]{2,1,0:T(8,128)(2,1)S(1)}, bf16[8,256,384]{2,1,0:T(8,128)(2,1)}, u32[]{:S(2)}) copy-start(bf16[8,256,384]{2,1,0:T(8,128)(2,1)} %copy.101) | copy-start | bytes 4718596
  707.3 6.4 copy-start.18
  707.3 6.4 copy-start.20
  709.0 5.1 copy-start.26
  709.0 5.1 copy-start.28
  709.0 35.8 %all-to-all-start.15 = ((bf16[256,8,384]{2,0,1:T(8,128)(2,1)}), bf16[256,8,384]{2,0,1:T(8,128)(2,1)}, u32[]{:S(2)}, u32[]{:S(2)}) async-start(bf16[256,8,384]{2,0,1:T(8,128)(2,1)} %copy.117), calls=%async_computation.16 | async-start | bytes 3145728 | tf_op jit(solution)/shard_map/all_to_all | solution.py:121
  715.8 2.0 copy-start.6
Sparse Core Ops, SparseCore 0:
  9.9 42.6 all-gather.9
  54.5 62.9 all-gather.11
  119.4 32.3 all-gather.13
  153.5 99.0 all-gather.17
  254.3 127.7 all-gather.15
  394.6 70.2 all-gather.19
  467.4 74.9 all-gather.21
  545.2 58.2 reduce-scatter.2
  606.9 49.3 reduce-scatter.4
  658.8 45.5 all-gather.23
  706.4 38.2 all-gather.25

commit v3 on v2

--- a/solution.py
+++ b/solution.py
@@ -192,11 +192,8 @@
     hidden_pre = jnp.dot(second_norm, inner_full, preferred_element_type=jnp.float32)
     hidden_act = smooth(hidden_pre).astype(jnp.bfloat16)
     outer_full = fetch_rows(mlp_out)
-    block_out = (second_mid.astype(jnp.float32) + late_sum(times_t(hidden_act, outer_full))).astype(
-        jnp.bfloat16
-    )
-    upstream_rows, first_own, second_own = lax.optimization_barrier(
-        (upstream_rows, own_columns(first_norm), own_columns(second_norm))
+    upstream_rows, second_own = lax.optimization_barrier(
+        (upstream_rows, own_columns(second_norm))
     )
     hidden_all = all_tokens(hidden_act)
     upstream_cols = lax.dynamic_slice_in_dim(
@@ -217,25 +214,32 @@
         local_frames,
     )
     triple_grad = temporal_back(temporal_grad)[0]
-    triple_grad, spatial_late = lax.optimization_barrier((triple_grad, spatial_output))
+    triple_grad, spatial_late, second_late = lax.optimization_barrier(
+        (triple_grad, spatial_output, second_grad_wide)
+    )
     triple_all = all_tokens(triple_grad)
     spatial_all = all_tokens(spatial_late)
-    back_terms, pre_all = lax.optimization_barrier(
-        (norm_back(first_wide, times_t(triple_grad, triple_full)).astype(jnp.bfloat16), pre_all)
-    )
-    first_back = head_sum(back_terms).astype(jnp.bfloat16)
+    first_back = head_sum(norm_back(first_wide, times_t(triple_grad, triple_full))).astype(
+        jnp.bfloat16
+    )
     first_grad = (
         second_grad.astype(jnp.float32) + to_frames(first_back, local_frames).astype(jnp.float32)
     ).astype(jnp.bfloat16)
-    first_grad_wide, triple_all = lax.optimization_barrier((widen(first_grad), triple_all))
+    first_grad, pre_all = lax.optimization_barrier((first_grad, pre_all))
+    first_grad_wide, triple_all, norm_late, hidden_late = lax.optimization_barrier(
+        (widen(first_grad), triple_all, first_norm, hidden_act)
+    )
+    block_out = (
+        second_mid.astype(jnp.float32) + late_sum(times_t(hidden_late, outer_full))
+    ).astype(jnp.bfloat16)
     spatial_grad = jnp.dot(
         first_grad_wide, spatial_full, preferred_element_type=jnp.float32
     ).astype(jnp.bfloat16)
     grad_spatial_qkv = spatial_back(spatial_grad)[0]
     grads = (
         left_times(own_columns(first_grad_wide), spatial_all),
-        left_times(first_own, triple_all),
-        send_rows(left_times(second_grad_wide, frames_result)),
+        left_times(own_columns(norm_late), triple_all),
+        send_rows(left_times(second_late, frames_result)),
         left_times(second_own, pre_all),
         left_times(upstream_own, hidden_all),
     )

time: 761 us -> 730 us (0.959)
  waiting for transfers between devices: 262 us -> 212 us
  blocking collectives: 243 us -> 262 us
  matrix products: 120 us -> 133 us
    all_gather x4, waiting for transfers between devices: 72 us -> 0.03 us  [all_tokens(): return lax.all_gather(table, 'seq', axis=0, tiled=True)]
    all_gather x5, waiting for transfers between devices: 8.81 us -> 51 us  [fetch_rows(): return lax.all_gather(weight, 'seq', axis=0, tiled=True)]
    all_to_all x2 -> x3, blocking collectives: 78.2 us -> 117 us  [widen(): lax.all_to_all(copies, 'fsdp', split_axis=0, concat_axis=2, tiled=True)[0]]
    all_to_all x4, waiting for transfers between devices: 82.7 us -> 51.1 us  [own_columns(): return lax.all_to_all(table, 'seq', split_axis=1, concat_axis=0, tiled=True)]
    all_to_all x3, blocking collectives: 150 us -> 119 us  [head_sum(): lax.all_to_all(terms.astype(jnp.bfloat16), 'fsdp', split_axis=1, concat_a...]
    reduce_scatter x1, waiting for transfers between devices: 0.02 us -> 27.5 us  [late_sum(): lax.psum_scatter(terms.astype(jnp.bfloat16), 'fsdp', scatter_dimension=1,...]
    all_to_all x2 -> x1, waiting for transfers between devices: 41.1 us -> 25 us  [widen(): lax.all_to_all(copies, 'fsdp', split_axis=0, concat_axis=2, tiled=True)[0]]
    all_to_all x1 -> x2, blocking collectives: 15.3 us -> 26.6 us  [regroup(): return lax.all_to_all(block, 'seq', split_axis=0, concat_axis=1, tiled=True)]
  transfers between devices with their start and end apart: 21 -> 19, of which waited for: 15 -> 10; matrix products, arithmetic and copies ran while one was open for 23% -> 26% of each run, Pallas kernels for 0% -> 0%
where the time goes in v3:
time: 730 us; the launch traced here: 728 us
  blocking collectives  262 us (36%)
  waiting for transfers between devices  212 us (29%)
  matrix products  133 us (18%)
  local copies, waits for them, and re-layouts  45.4 us (6%)
  starting transfers between devices  36.1 us (5%)
  other arithmetic  23.8 us (3%)
  between operations  14.8 us (2%)
    all_to_all x3, blocking collectives, head_sum(): lax.all_to_all(terms.astype(jnp.bfloat16), 'fsdp', split_axis=1, concat_a...  119 us
    all_to_all x3, blocking collectives, widen(): lax.all_to_all(copies, 'fsdp', split_axis=0, concat_axis=2, tiled=True)[0]  117 us
    all_to_all x4, waiting for transfers between devices, own_columns(): return lax.all_to_all(table, 'seq', split_axis=1, concat_axis=0, tiled=True)  51.1 us
    all_gather x5, waiting for transfers between devices, fetch_rows(): return lax.all_gather(weight, 'seq', axis=0, tiled=True)  51 us
    dot_general x5, matrix products, times_t(): lax.dot_general(matrix, factor, (((1,), (1,)), ((), ())), preferred_eleme...  38.7 us
    all_to_all x1, waiting for transfers between devices, head_sum(): lax.all_to_all(terms.astype(jnp.bfloat16), 'fsdp', split_axis=1, concat_a...  37.6 us
    dot_general x5, matrix products, left_times(): lax.dot_general(matrix, factor, (((0,), (0,)), ((), ())), preferred_eleme...  36.2 us
    reduce_scatter x1, waiting for transfers between devices, late_sum(): lax.psum_scatter(terms.astype(jnp.bfloat16), 'fsdp', scatter_dimension=1,...  27.5 us
  transfers between devices with their start and end apart: 19, of which 10 were waited for; matrix products, arithmetic and copies ran while one was open for 26% of the time, Pallas kernels for 0%

profile of v3, /device:TPU:0, one launch (start us, length us, event | category | flops | bytes accessed | tf_op | source)
XLA Modules:
  0.0 727.7 jit_solution(3166429611644507811)
XLA Ops:
  10.6 1.6 copy.83
  12.1 5.2 all-to-all-start
  19.9 22.6 %all-to-all-done = bf16[256,8,384]{0,2,1:T(8,128)(2,1)S(1)} async-done(((bf16[256,8,384]{0,2,1:T(8,128)(2,1)}), bf16[256,8,384]{0,2,1:T(8,128)(2,1)S(1)}, u32[]{:S(2)}, u32[]{:S(2)}) %all-to-all-start) | async-done | bytes 1572896 | tf_op jit(solution)/shard_map/all_to_all | solution.py:121
  42.5 1.6 copy.84
  44.1 8.5 %all-gather.10.cloned.1.call-done = bf16[3072,512]{1,0:T(8,128)(2,1)} async-done(((bf16[384,512]{1,0:T(8,128)(2,1)}), bf16[3072,512]{1,0:T(8,128)(2,1)}) %all-gather.10.cloned.1.call-update) | async-done | bytes 3145744 | tf_op jit(solution)/shard_map/all_gather | solution.py:96
  52.6 2.9 convolution_convert_fusion.2
  55.7 42.2 %all_to_all.209 = bf16[256,4,768]{2,0,1:T(8,128)(2,1)S(1)} all-to-all(bf16[256,4,768]{2,0,1:T(8,128)(2,1)S(1)} %bitcast.233), channel_id=1, replica_groups=mesh['seq'=8,'fsdp'=4] {'fsdp'}, dimensions={1} | all-to-all | bytes 3145728 | tf_op jit(solution)/shard_map/all_to_all | solution.py:106
  98.2 15.3 %all_to_all.210 = bf16[8,1,32,768]{3,2,1,0:T(8,128)(2,1)S(1)} all-to-all(bf16[8,1,32,768]{3,2,1,0:T(8,128)(2,1)S(1)} %add_convert_fusion.3), channel_id=1, replica_groups=mesh['seq'=8,'fsdp'=4] {'seq'}, dimensions={0} | all-to-all | bytes 786432 | tf_op jit(solution)/shard_map/all_to_all | solution.py:135
  113.6 39.0 %all_to_all.211 = bf16[4,256,768]{2,1,0:T(8,128)(2,1)S(1)} all-to-all(bf16[4,256,768]{2,1,0:T(8,128)(2,1)S(1)} %broadcast_in_dim.35), channel_id=1, replica_groups=mesh['seq'=8,'fsdp'=4] {'fsdp'}, dimensions={0} | all-to-all | bytes 3145728 | tf_op jit(solution)/shard_map/all_to_all | solution.py:101
  152.9 2.0 copy.88
  156.4 1.7 fusion.14
  158.0 9.0 %convolution_convert_fusion.3 = bf16[256,1536]{1,0:T(8,128)(2,1)} fusion(bf16[256,3072]{1,0:T(8,128)(2,1)} %fusion.14, bf16[3072,1536]{1,0:T(8,128)(2,1)} %all-gather.12.cloned.1.call-done), kind=kOutput, calls=%fused_computation.38 | convolution fusion | flops 2416312320 | bytes 11796480 | tf_op jit(solution)/shard_map/dot_general | solution.py:178
  167.1 3.6 reshape.270
  170.6 3.8 fusion.54
  177.5 2.9 fusion.58
  180.4 1.5 convolution_convert_fusion.14
  182.7 1.8 reshape.272
  184.5 4.0 all-to-all-start.4
  188.5 6.9 all-to-all-done.4
  195.5 3.0 convolution_convert_fusion.1
  198.6 39.3 %all_to_all.212 = bf16[256,4,768]{2,0,1:T(8,128)(2,1)S(1)} all-to-all(bf16[256,4,768]{2,0,1:T(8,128)(2,1)S(1)} %bitcast.234), channel_id=1, replica_groups=mesh['seq'=8,'fsdp'=4] {'fsdp'}, dimensions={1} | all-to-all | bytes 3145728 | tf_op jit(solution)/shard_map/all_to_all | solution.py:106
  241.2 38.4 %all_to_all.213 = bf16[4,256,768]{1,2,0:T(8,128)(2,1)S(1)} all-to-all(bf16[4,256,768]{1,2,0:T(8,128)(2,1)S(1)} %broadcast_in_dim.37), channel_id=1, replica_groups=mesh['seq'=8,'fsdp'=4] {'fsdp'}, dimensions={0} | all-to-all | bytes 3145728 | tf_op jit(solution)/shard_map/all_to_all | solution.py:101
  281.5 1.6 multiply_convert_fusion.4
  283.2 4.3 all-to-all-start.7
  287.5 3.5 copy.127
  291.1 21.0 %all-to-all-done.7 = bf16[256,8,384]{0,2,1:T(8,128)(2,1)} async-done(((bf16[256,8,384]{0,2,1:T(8,128)(2,1)}), bf16[256,8,384]{0,2,1:T(8,128)(2,1)}, u32[]{:S(2)}, u32[]{:S(2)}) %all-to-all-start.7) | async-done | bytes 1572896 | tf_op jit(solution)/shard_map/all_to_all | solution.py:121
  312.1 2.7 copy.97
  314.8 13.0 %fusion.59 = f32[256,3072]{1,0:T(8,128)} fusion(bf16[256,3072]{1,0:T(8,128)(2,1)} %bitcast.243, bf16[3072,3072]{1,0:T(8,128)(2,1)} %all-gather.16.cloned.1.call-done), kind=kOutput, calls=%fused_computation.131 | convolution fusion | flops 4831838208 | bytes 23592960 | tf_op jit(solution)/shard_map/dot_general | solution.py:202
  327.7 42.4 %all-gather.18.cloned.1.call-done = bf16[3072,3072]{1,0:T(8,128)(2,1)} async-done(((bf16[384,3072]{1,0:T(8,128)(2,1)}), bf16[3072,3072]{1,0:T(8,128)(2,1)}) %all-gather.18.cloned.1.call-update) | async-done | bytes 18874384 | tf_op jit(solution)/shard_map/all_gather | solution.py:96
  370.2 13.4 %multiply_convert_fusion.2 = (bf16[256,3072]{1,0:T(8,128)(2,1)}, bf16[256,3072]{1,0:T(8,128)(2,1)}) fusion(f32[256,3072]{1,0:T(8,128)} %fusion.59, bf16[3072,3072]{1,0:T(8,128)(2,1)} %all-gather.18.cloned.1.call-done, f32[256,3072]{1,0:T(8,128)} %copy.127, f32[256]{0:T(256)S(1)} %broadcast_multiply_fusion.4, f32[256]{0:T(256)S(1)} %add_rsqrt_fusion), kind=kOutput, calls=%fused_computation.28 | convolution fusion | flops 4851499008 | bytes 28313600 | tf_op jit(solution)/shard_map/dot_general | solution.py:192
  384.3 13.2 %fusion.53 = (f32[256]{0:T(256)S(1)}, f32[256]{0:T(256)S(1)}, f32[256,3072]{1,0:T(8,128)}) fusion(f32[256]{0:T(256)S(1)} %add_rsqrt_fusion, f32[256,3072]{1,0:T(8,128)} %copy.127, f32[256]{0:T(256)S(1)} %broadcast_multiply_fusion.4, bf16[256,3072]{1,0:T(8,128)(2,1)} %get-tuple-element.75, bf16[3072,3072]{1,0:T(8,128)(2,1)} %all-gather.18.cloned.1.call-done), kind=kOutput, calls=%fused_computation.125 | convolution fusion | flops 4835770368 | bytes 26742784 | tf_op jit(solution)/shard_map/dot_general | solution.py:34
  397.6 3.1 multiply_convert_fusion.3
  401.9 4.6 all-to-all-start.8
  406.6 37.6 %all-to-all-done.8 = bf16[256,4,768]{2,0,1:T(8,128)(2,1)} async-done(((bf16[256,4,768]{2,0,1:T(8,128)(2,1)}), bf16[256,4,768]{2,0,1:T(8,128)(2,1)}, u32[]{:S(2)}, u32[]{:S(2)}) %all-to-all-start.8) | async-done | bytes 1572896 | tf_op jit(solution)/shard_map/all_to_all | solution.py:106
  444.2 1.7 convert_reduce_fusion.1
  449.1 39.8 %all_to_all.214 = bf16[4,256,768]{1,2,0:T(8,128)(2,1)} all-to-all(bf16[4,256,768]{1,2,0:T(8,128)(2,1)S(1)} %broadcast_in_dim.38), channel_id=1, replica_groups=mesh['seq'=8,'fsdp'=4] {'fsdp'}, dimensions={0} | all-to-all | bytes 3145728 | tf_op jit(solution)/shard_map/all_to_all | solution.py:101
  488.9 4.1 convolution_convert_fusion.13
  493.0 4.0 all-to-all-start.10
  498.6 8.5 %all-to-all-done.10 = bf16[8,1,32,512]{3,2,1,0:T(8,128)(2,1)} async-done(((bf16[8,1,32,512]{3,2,1,0:T(8,128)(2,1)}), bf16[8,1,32,512]{3,2,1,0:T(8,128)(2,1)}, u32[]{:S(2)}, u32[]{:S(2)}) %all-to-all-start.10) | async-done | bytes 262176 | tf_op jit(solution)/shard_map/all_to_all | solution.py:135
  507.1 1.7 reshape_reshape.3
  510.2 1.5 multiply_reduce_fusion.2
  513.8 1.6 copy.158
  515.4 3.2 reshape.276
  518.7 8.9 %fusion.52 = (f32[256]{0:T(256)}, f32[256]{0:T(256)S(1)}, f32[256,3072]{1,0:T(8,128)}) fusion(f32[256]{0:T(256)S(1)} %add_rsqrt_fusion.1, f32[256,3072]{1,0:T(8,128)S(1)} %bitcast.216, f32[256]{0:T(256)S(1)} %broadcast_multiply_fusion.5, bf16[256,1536]{1,0:T(8,128)(2,1)} %reshape.276, bf16[3072,1536]{1,0:T(8,128)(2,1)} %all-gather.12.cloned.1.call-done), kind=kOutput, calls=%fused_computation.124 | convolution fusion | flops 2419850752 | bytes 16519168 | tf_op jit(solution)/shard_map/dot_general | solution.py:34
  527.7 3.6 multiply_convert_fusion
  532.0 3.0 multiply_convert_fusion.1
  535.1 37.1 %all_to_all.215 = bf16[256,4,768]{2,0,1:T(8,128)(2,1)S(1)} all-to-all(bf16[256,4,768]{2,0,1:T(8,128)(2,1)S(1)} %bitcast.235), channel_id=1, replica_groups=mesh['seq'=8,'fsdp'=4] {'fsdp'}, dimensions={1} | all-to-all | bytes 3145728 | tf_op jit(solution)/shard_map/all_to_all | solution.py:106
  572.6 11.3 %all_to_all.216 = bf16[8,1,32,768]{3,2,1,0:T(8,128)(2,1)S(1)} all-to-all(bf16[8,1,32,768]{3,2,1,0:T(8,128)(2,1)S(1)} %bitcast.248), channel_id=1, replica_groups=mesh['seq'=8,'fsdp'=4] {'seq'}, dimensions={0} | all-to-all | bytes 786432 | tf_op jit(solution)/shard_map/all_to_all | solution.py:135
  585.6 4.6 all-to-all-start.13
  590.8 10.8 %convolution_multiply_fusion = f32[384,3072]{1,0:T(8,128)} fusion(bf16[2048,384]{1,0:T(8,128)(2,1)S(1)} %bitcast.224, bf16[2048,3072]{1,0:T(8,128)(2,1)} %all-gather.20.cloned.1.call-done), kind=kOutput, calls=%fused_computation.8 | convolution fusion | flops 4833017856 | bytes 18874368 | tf_op jit(solution)/shard_map/dot_general | solution.py:41
  601.6 25.0 %all-to-all-done.13 = bf16[4,256,768]{1,2,0:T(8,128)(2,1)S(1)} async-done(((bf16[4,256,768]{1,2,0:T(8,128)(2,1)}), bf16[4,256,768]{1,2,0:T(8,128)(2,1)S(1)}, u32[]{:S(2)}, u32[]{:S(2)}) %all-to-all-start.13) | async-done | bytes 1572896 | tf_op jit(solution)/shard_map/all_to_all | solution.py:101
  626.6 1.7 copy.114
  628.3 4.3 all-to-all-start.14
  632.7 10.6 %convolution_convert_fusion = bf16[256,3072]{1,0:T(8,128)(2,1)} fusion(bf16[256,3072]{1,0:T(8,128)(2,1)} %get-tuple-element.28, bf16[3072,3072]{1,0:T(8,128)(2,1)} %all-gather.16.cloned.1.call-done), kind=kOutput, calls=%fused_computation.10 | convolution fusion | flops 4832624640 | bytes 22020096 | tf_op jit(solution)/shard_map/dot_general | solution.py:34
  643.3 10.9 %convolution_multiply_fusion.1 = f32[384,3072]{1,0:T(8,128)} fusion(bf16[2048,384]{1,0:T(8,128)(2,1)S(1)} %bitcast.225, bf16[2048,3072]{1,0:T(8,128)(2,1)} %all-gather.22.cloned.1.call-done), kind=kOutput, calls=%fused_computation.9 | convolution fusion | flops 4833017856 | bytes 18874368 | tf_op jit(solution)/shard_map/dot_general | solution.py:41
  654.3 2.0 convert_element_type.292
  657.5 4.2 all-to-all-start.15
  661.8 3.5 convolution_convert_fusion.8
  666.4 2.2 fusion.29
  673.2 4.0 convolution_multiply_fusion.4
  677.1 7.5 %all-to-all-done.15 = bf16[256,8,384]{2,0,1:T(8,128)(2,1)S(1)} async-done(((bf16[256,8,384]{2,0,1:T(8,128)(2,1)}), bf16[256,8,384]{2,0,1:T(8,128)(2,1)S(1)}, u32[]{:S(2)}, u32[]{:S(2)}) %all-to-all-start.15) | async-done | bytes 1572896 | tf_op jit(solution)/shard_map/all_to_all | solution.py:121
  684.6 7.0 convolution_multiply_fusion.2
  691.6 27.5 %reduce-scatter.3.cloned.1.call-done = bf16[256,768]{1,0:T(8,128)(2,1)} async-done(((bf16[256,3072]{1,0:T(8,128)(2,1)}), bf16[256,768]{1,0:T(8,128)(2,1)}) %reduce-scatter.3.cloned.1.call-update) | async-done | bytes 393232 | tf_op jit(solution)/shard_map/reduce_scatter | solution.py:115
  719.1 1.9 fusion.40
  (148 shorter events, 37.8 us)
Async XLA Ops:
  7.2 45.4 %all-gather.10.cloned.1.call-start = ((), (), s32[]{:S(2)}) async-start(), calls=%async_computation.18 | async-start | bytes 3538944 | tf_op jit(solution)/shard_map/all_gather | solution.py:96
  7.9 2.7 copy-start.13
  7.9 150.1 %all-gather.12.cloned.1.call-start = ((), (), s32[]{:S(2)}) async-start(), calls=%async_computation.19 | async-start | bytes 10616832 | tf_op jit(solution)/shard_map/all_gather | solution.py:96
  8.7 179.9 %all-gather.14.cloned.1.call-start = ((), (), s32[]{:S(2)}) async-start(), calls=%async_computation.20 | async-start | bytes 3538944 | tf_op jit(solution)/shard_map/all_gather | solution.py:96
  9.4 305.4 %all-gather.16.cloned.1.call-start = ((), (), s32[]{:S(2)}) async-start(), calls=%async_computation.21 | async-start | bytes 21233664 | tf_op jit(solution)/shard_map/all_gather | solution.py:96
  10.0 360.2 %all-gather.18.cloned.1.call-start = ((), (), s32[]{:S(2)}) async-start(), calls=%async_computation.22 | async-start | bytes 21233664 | tf_op jit(solution)/shard_map/all_gather | solution.py:96
  10.6 6.8 copy-start.20
  12.1 30.4 %all-to-all-start = ((bf16[256,8,384]{0,2,1:T(8,128)(2,1)}), bf16[256,8,384]{0,2,1:T(8,128)(2,1)S(1)}, u32[]{:S(2)}, u32[]{:S(2)}) async-start(bf16[256,8,384]{0,2,1:T(8,128)(2,1)} %bitcast.7), calls=%async_computation | async-start | bytes 3145728 | tf_op jit(solution)/shard_map/all_to_all | solution.py:121
  17.6 2.2 copy-start.18
  17.6 2.2 copy-start.25
  17.6 2.2 copy-start.27
  19.9 35.7 %copy-start.16 = (bf16[4,256,128]{1,2,0:T(8,128)(2,1)}, bf16[4,256,128]{1,2,0:T(8,128)(2,1)S(1)}, u32[]{:S(2)}) copy-start(bf16[4,256,128]{1,2,0:T(8,128)(2,1)S(1)} %convolution_convert_fusion.15) | copy-start | bytes 786436
  55.7 42.4 %copy-start.11 = (bf16[1,256,768]{2,1,0:T(8,128)(2,1)S(1)}, bf16[1,256,768]{2,1,0:T(8,128)(2,1)}, u32[]{:S(2)}) copy-start(bf16[1,256,768]{2,1,0:T(8,128)(2,1)} %param.8) | copy-start | bytes 1179652
  98.1 15.5 %copy-start.2 = (f32[256,768]{1,0:T(8,128)}, f32[256,768]{1,0:T(8,128)S(1)}, u32[]{:S(2)}) copy-start(f32[256,768]{1,0:T(8,128)S(1)} %convert_reduce_fusion.3) | copy-start | bytes 2359300
  184.5 11.0 %all-to-all-start.4 = ((bf16[8,1,32,512]{3,2,1,0:T(8,128)(2,1)}), bf16[8,1,32,512]{3,2,1,0:T(8,128)(2,1)}, u32[]{:S(2)}, u32[]{:S(2)}) async-start(bf16[8,1,32,512]{3,2,1,0:T(8,128)(2,1)} %bitcast.254), calls=%async_computation.4 | async-start | bytes 524288 | tf_op jit(solution)/shard_map/all_to_all | solution.py:135
  198.6 40.5 %copy-start.3 = (f32[256,768]{1,0:T(8,128)S(1)}, f32[256,768]{1,0:T(8,128)}, u32[]{:S(2)}) copy-start(f32[256,768]{1,0:T(8,128)} %copy-done.2) | copy-start | bytes 2359300
  238.2 0.9 copy-start.5
  279.9 1.7 copy-start
  283.2 28.9 %all-to-all-start.7 = ((bf16[256,8,384]{0,2,1:T(8,128)(2,1)}), bf16[256,8,384]{0,2,1:T(8,128)(2,1)}, u32[]{:S(2)}, u32[]{:S(2)}) async-start(bf16[256,8,384]{0,2,1:T(8,128)(2,1)} %multiply_convert_fusion.4), calls=%async_computation.7 | async-start | bytes 3145728 | tf_op jit(solution)/shard_map/all_to_all | solution.py:121
  287.5 201.4 %all-gather.20.cloned.1.call-start = ((), (), s32[]{:S(2)}) async-start(), calls=%async_computation.23 | async-start | bytes 14155776 | tf_op jit(solution)/shard_map/all_gather | solution.py:125
  383.6 200.6 %all-gather.22.cloned.1.call-start = ((), (), s32[]{:S(2)}) async-start(), calls=%async_computation.24 | async-start | bytes 14155776 | tf_op jit(solution)/shard_map/all_gather | solution.py:125
  384.3 13.3 %copy-start.1 = (f32[256,3072]{1,0:T(8,128)S(1)}, f32[256,3072]{1,0:T(8,128)}, u32[]{:S(2)}) copy-start(f32[256,3072]{1,0:T(8,128)} %copy.127) | copy-start | bytes 9437188
  401.9 42.3 %all-to-all-start.8 = ((bf16[256,4,768]{2,0,1:T(8,128)(2,1)}), bf16[256,4,768]{2,0,1:T(8,128)(2,1)}, u32[]{:S(2)}, u32[]{:S(2)}) async-start(bf16[256,4,768]{2,0,1:T(8,128)(2,1)} %bitcast.230), calls=%async_computation.8 | async-start | bytes 3145728 | tf_op jit(solution)/shard_map/all_to_all | solution.py:106
  493.0 14.1 %all-to-all-start.10 = ((bf16[8,1,32,512]{3,2,1,0:T(8,128)(2,1)}), bf16[8,1,32,512]{3,2,1,0:T(8,128)(2,1)}, u32[]{:S(2)}, u32[]{:S(2)}) async-start(bf16[8,1,32,512]{3,2,1,0:T(8,128)(2,1)} %bitcast.264), calls=%async_computation.10 | async-start | bytes 524288 | tf_op jit(solution)/shard_map/all_to_all | solution.py:135
  497.0 129.6 %all-gather.24.cloned.1.call-start = ((), (), s32[]{:S(2)}) async-start(), calls=%async_computation.25 | async-start | bytes 7077888 | tf_op jit(solution)/shard_map/all_gather | solution.py:125
  508.8 4.2 copy-start.21
  508.8 4.2 copy-start.23
  508.8 4.2 copy-start.29
  510.2 3.2 copy-start.24
  518.7 135.6 %reduce-scatter.5.cloned.1.call-start = ((), (), s32[]{:S(2)}) async-start(), calls=%async_computation.28 | async-start | bytes 3538944 | tf_op jit(solution)/shard_map/reduce_scatter | solution.py:129
  518.7 9.0 %copy-start.14 = (bf16[4,256,768]{1,2,0:T(8,128)(2,1)S(1)}, bf16[4,256,768]{1,2,0:T(8,128)(2,1)}, u32[]{:S(2)}) copy-start(bf16[4,256,768]{1,2,0:T(8,128)(2,1)} %all_to_all.214) | copy-start | bytes 4718596
  584.1 1.5 copy-start.15
  584.1 6.6 copy-start.7
  585.6 41.0 %all-to-all-start.13 = ((bf16[4,256,768]{1,2,0:T(8,128)(2,1)}), bf16[4,256,768]{1,2,0:T(8,128)(2,1)S(1)}, u32[]{:S(2)}, u32[]{:S(2)}) async-start(bf16[4,256,768]{1,2,0:T(8,128)(2,1)} %broadcast_in_dim.85), calls=%async_computation.13 | async-start | bytes 3145728 | tf_op jit(solution)/shard_map/all_to_all | solution.py:101
  590.2 83.0 %all-gather.26.cloned.1.call-start = ((), (), s32[]{:S(2)}) async-start(), calls=%async_computation.27 | async-start | bytes 2359296 | tf_op jit(solution)/shard_map/all_gather | solution.py:125
  626.6 1.7 copy-start.9
  628.3 29.2 %all-to-all-start.14 = ((bf16[256,8,384]{2,0,1:T(8,128)(2,1)}), bf16[256,8,384]{2,0,1:T(8,128)(2,1)}, u32[]{:S(2)}, u32[]{:S(2)}) async-start(bf16[256,8,384]{2,0,1:T(8,128)(2,1)} %copy.114), calls=%async_computation.15 | async-start | bytes 3145728 | tf_op jit(solution)/shard_map/all_to_all | solution.py:121
  632.6 10.7 %copy-start.8 = (bf16[8,256,384]{2,1,0:T(8,128)(2,1)S(1)}, bf16[8,256,384]{2,1,0:T(8,128)(2,1)}, u32[]{:S(2)}) copy-start(bf16[8,256,384]{2,1,0:T(8,128)(2,1)} %copy.97) | copy-start | bytes 4718596
  632.6 86.5 %reduce-scatter.3.cloned.1.call-start = ((), (), s32[]{:S(2)}) async-start(), calls=%async_computation.26 | async-start | bytes 1966080 | tf_op jit(solution)/shard_map/reduce_scatter | solution.py:115
  643.3 12.9 %copy-start.10 = (bf16[256,3072]{1,0:T(8,128)(2,1)S(1)}, bf16[256,3072]{1,0:T(8,128)(2,1)}, u32[]{:S(2)}) copy-start(bf16[256,3072]{1,0:T(8,128)(2,1)} %fusion.14) | copy-start | bytes 4718596
  657.5 27.1 %all-to-all-start.15 = ((bf16[256,8,384]{2,0,1:T(8,128)(2,1)}), bf16[256,8,384]{2,0,1:T(8,128)(2,1)S(1)}, u32[]{:S(2)}, u32[]{:S(2)}) async-start(bf16[256,8,384]{2,0,1:T(8,128)(2,1)} %bitcast.228), calls=%async_computation.16 | async-start | bytes 3145728 | tf_op jit(solution)/shard_map/all_to_all | solution.py:121
  661.7 3.6 copy-start.17
  661.8 3.6 copy-start.19
  666.4 2.2 copy-start.22
  666.4 2.2 copy-start.26
  666.4 2.2 copy-start.28
  684.6 34.5 %copy-start.4 = (f32[256,768]{1,0:T(8,128)S(1)}, f32[256,768]{1,0:T(8,128)}, u32[]{:S(2)}) copy-start(f32[256,768]{1,0:T(8,128)} %copy-done.2) | copy-start | bytes 2359300
  684.6 34.5 %copy-start.6 = (f32[256,768]{1,0:T(8,128)S(1)}, f32[256,768]{1,0:T(8,128)}, u32[]{:S(2)}) copy-start(f32[256,768]{1,0:T(8,128)} %copy-done.5) | copy-start | bytes 2359300
  684.6 34.5 %copy-start.12 = (bf16[1,256,768]{2,1,0:T(8,128)(2,1)S(1)}, bf16[1,256,768]{2,1,0:T(8,128)(2,1)}, u32[]{:S(2)}) copy-start(bf16[1,256,768]{2,1,0:T(8,128)(2,1)} %param.8) | copy-start | bytes 1179652
Sparse Core Ops, SparseCore 0:
  9.9 42.6 all-gather.9
  54.5 62.9 all-gather.11
  119.4 32.3 all-gather.13
  153.5 101.5 all-gather.15
  256.8 113.2 all-gather.17
  383.7 72.1 all-gather.19
  457.7 74.9 all-gather.21
  535.2 45.5 all-gather.23
  584.1 50.3 reduce-scatter.4
  636.4 34.2 all-gather.25
  673.1 45.9 reduce-scatter.2
